TPU v7x, 256 devices: a whole 4x4x8 slice. The times are simulated.
256 devices in a mesh: region: 64 (over x, z, core), mode: 4 (over y).
Axes of the slice: x: 4, y: 4, z: 8, core: 2. Of those that a mesh axis runs over, the one named last changes fastest.
Arguments:
- modes: bfloat16 [6, 64, 262144], P(None, 'mode', 'region'), may hold values from -1.1953125 to 1.1953125
- stiffness: bfloat16 [6, 4, 6, 4, 262144], P(None, None, None, None, 'region'), may hold values from -1.25 to 1.25
- mass_ref: bfloat16 [6, 4, 6, 4], replicated, may hold values from -1.25 to 1.25
- areas: float32 [262144], P('region'), may hold values from 0.5 to 2
- eigenvalues: float32 [64], P('mode'), may hold values from 0.5 to 4
- send_list: int32 [4, 8192], P(None, 'region'), may hold values from 0 to 4095, as said below
- connect: int32 [4, 262144], P(None, 'region'), may hold values from 0 to 4607, as said below
- block_var: int32 [8192], P('region'), may hold values from 0 to 8191, as said below
- mode_weight: float32 [64], P('mode'), may hold values from 0.25 to 4
Outputs:
- sens: float32 [64, 8192], P('mode', 'region')
- aggregate: float32 [8192], P('region')
Inputs may be any that keep to these rules, and one draw needn't show every extreme that they name: `send_list`: each region's list for one direction names 128 distinct local nodes. `connect`: A number below 4096 is an owned node; 4096 + d * 128 + s is entry s of direction d in the extended list, used only where region r - o_d exists. `block_var`: A block of region r names a variable v with v // 128 in r - 1, r, r + 1.
All inputs are finite; a program needn't handle non-finite values.
Results may differ from a plain program's by a relative error of at most 0.0003.
Values may be sent and summed in bfloat16 or wider, within the bound.
No kernel may reach another device: no remote copies, remote signals or barrier semaphores. Data moves between devices by JAX's collectives and lax.ppermute only.
A program may use at most 192 MiB of HBM per device.

v0:
```python
import jax
import jax.numpy as jnp
from jax import lax
from jax.sharding import PartitionSpec as P

BLOCK = 32
VAR_DEV = 128


OFFSETS = (1, -1, 2, -2)


def shifted(array, axis, by):
    length = lax.axis_size(axis)
    pairs = [(i, i + by) for i in range(length) if 0 <= i + by < length]
    return lax.ppermute(array, axis, pairs)


def shards(
    modes, stiffness, mass_ref, areas, eigenvalues, send_list, connect, block_var, mode_weight
):
    region_id = lax.axis_index("region")
    mode_dev = modes.shape[1]
    node_count = modes.shape[2]
    elem_count = connect.shape[1]
    flat_modes = modes.reshape(6 * mode_dev, node_count)
    outgoing = [jnp.take(flat_modes, send_list[direction], axis=1) for direction in range(4)]
    ghosts = [
        shifted(outgoing[direction], "region", offset) for direction, offset in enumerate(OFFSETS)
    ]
    extended = jnp.concatenate([flat_modes] + ghosts, axis=1)
    corner_rows = [
        jnp.take(extended, connect[corner], axis=1).reshape(6, mode_dev, elem_count)
        for corner in range(4)
    ]
    element_rows = jnp.stack(corner_rows, axis=1).reshape(24, mode_dev, elem_count)
    stiff_flat = stiffness.reshape(24, 24, elem_count)
    coupled = jnp.einsum(
        "imE,ijE->jmE", element_rows, stiff_flat, preferred_element_type=jnp.float32
    )
    stiff_part = jnp.sum(element_rows * coupled, axis=0)
    mass_flat = mass_ref.reshape(24, 24)
    mass_rows = lax.dot_general(
        mass_flat,
        element_rows.reshape(24, mode_dev * elem_count),
        (((0,), (0,)), ((), ())),
        preferred_element_type=jnp.float32,
    )
    mass_part = jnp.sum(mass_rows.reshape(24, mode_dev, elem_count) * element_rows, axis=0)
    energy = stiff_part - eigenvalues[:, None] * areas[None, :] * mass_part
    column = jnp.repeat(block_var - (region_id - 1) * VAR_DEV, BLOCK)
    table = (column[:, None] == jnp.arange(3 * VAR_DEV, dtype=jnp.int32)[None, :]).astype(
        jnp.float32
    )
    window = jnp.dot(energy, table, precision=lax.Precision.HIGHEST)
    sens = window[:, VAR_DEV : 2 * VAR_DEV]
    for step_by, first in ((1, 2 * VAR_DEV), (-1, 0)):
        sens = sens + shifted(window[:, first : first + VAR_DEV], "region", step_by)
    weighted = jnp.dot(mode_weight, sens, precision=lax.Precision.HIGHEST)
    aggregate = lax.psum(weighted, "mode")
    return (sens, aggregate)


def solution(mesh):
    in_specs = (
        P(None, "mode", "region"),
        P(None, None, None, None, "region"),
        P(),
        P("region"),
        P("mode"),
        P(None, "region"),
        P(None, "region"),
        P("region"),
        P("mode"),
    )
    out_specs = (P("mode", "region"), P("region"))
    return jax.shard_map(shards, mesh=mesh, in_specs=in_specs, out_specs=out_specs, check_vma=False)
```

profile of v0, /device:TPU:6, one launch (start us, length us, event | category | flops | bytes accessed | tf_op | source)
XLA Modules:
  0.0 211.4 jit_solution(5236545207839266186)
XLA Ops:
  0.6 0.0 copy-start
  0.6 0.0 copy-start.2
  0.7 0.0 copy-start.6
  0.7 0.8 compare_and_fusion.4
  1.5 1.6 copy.77
  3.1 0.7 gather_fusion
  3.8 0.1 select_bitcast_fusion.7
  3.9 1.9 collective-permute-start
  5.9 0.7 gather_fusion.1
  6.6 0.1 select_bitcast_fusion.6
  6.7 7.5 %collective-permute-start.1 = (bf16[96,128]{0,1:T(8,128)(2,1)S(1)}, bf16[96,128]{0,1:T(8,128)(2,1)S(1)}, u32[]{:S(2)}, u32[]{:S(2)}) collective-permute-start(bf16[96,128]{0,1:T(8,128)(2,1)S(1)} %select_bitcast_fusion.6), channel_id=1, source_target_pairs={{4,0},{8,4},{12,8},{16,12},{20,16},{24,20},{28,24},{32,28},{36,32}... | collective-permute-start | bytes 73736 | tf_op jit(solution)/shard_map/ppermute | solution.py:16
  14.2 0.7 gather_fusion.2
  14.9 0.1 select_bitcast_fusion.5
  15.0 1.9 collective-permute-start.2
  16.9 0.7 gather_fusion.3
  17.6 0.1 select_bitcast_fusion.4
  17.7 6.0 %collective-permute-start.3 = (bf16[96,128]{0,1:T(8,128)(2,1)S(1)}, bf16[96,128]{0,1:T(8,128)(2,1)S(1)}, u32[]{:S(2)}, u32[]{:S(2)}) collective-permute-start(bf16[96,128]{0,1:T(8,128)(2,1)S(1)} %select_bitcast_fusion.4), channel_id=1, source_target_pairs={{8,0},{12,4},{16,8},{20,12},{24,16},{28,20},{32,24},{36,28},{40,32... | collective-permute-start | bytes 73736 | tf_op jit(solution)/shard_map/ppermute | solution.py:16
  23.7 0.1 constant_dynamic-update-slice_fusion.4
  23.8 0.0 copy-done.2
  24.0 0.0 copy-done.6
  24.0 7.7 %reshape.34 = bf16[24,24,4096]{2,1,0:T(8,128)(2,1)} reshape(bf16[6,4,6,4,4096]{4,3,2,1,0:T(4,128)(2,1)} %param.14) | data formatting | bytes 9437184 | tf_op jit(solution)/shard_map/reshape | solution.py:37
  31.7 23.2 %copy.84 = bf16[24,24,4096]{1,0,2:T(8,128)(2,1)} copy(bf16[24,24,4096]{2,1,0:T(8,128)(2,1)} %reshape.34) | data formatting | bytes 9437184 | tf_op jit(solution)/shard_map/reshape | solution.py:37
  54.9 0.0 copy-done.4
  54.9 0.3 copy.88
  55.2 0.1 reshape.35
  55.3 0.1 broadcast_in_dim.24
  55.4 0.1 eq.15
  55.5 0.0 collective-permute-done
  55.5 0.0 collective-permute-done.1
  55.5 0.0 collective-permute-done.2
  55.5 0.0 collective-permute-done.3
  55.6 12.1 %gather_fusion.4 = bf16[4096,96]{1,0:T(8,128)(2,1)S(1)} fusion(bf16[96,4608]{0,1:T(8,128)(2,1)S(1)} %constant_dynamic-update-slice_fusion, s32[4096]{0:T(1024)S(1)} %get-tuple-element.24), kind=kCustom, calls=%fused_computation.1.clone | custom fusion | bytes 1589248 | tf_op jit(solution)/shard_map/jit(_take)/gather | solution.py:33
  67.7 2.1 %select_bitcast_fusion.3 = bf16[96,4096]{0,1:T(8,128)(2,1)S(1)} fusion(bf16[4096,96]{1,0:T(8,128)(2,1)S(1)} %gather_fusion.4, pred[4096]{0:T(1024)(128)(4,1)S(1)} %compare_and_fusion.3), kind=kLoop, calls=%fused_computation.21 | loop fusion | flops 393216 | bytes 1576960 | tf_op jit(solution)/shard_map/jit(_take)/select_n | solution.py:33
  69.9 1.3 copy.78
  71.1 12.1 %gather_fusion.5 = bf16[4096,96]{1,0:T(8,128)(2,1)S(1)} fusion(bf16[96,4608]{0,1:T(8,128)(2,1)S(1)} %constant_dynamic-update-slice_fusion, s32[4096]{0:T(1024)S(1)} %get-tuple-element.25), kind=kCustom, calls=%fused_computation.5.clone | custom fusion | bytes 1589248 | tf_op jit(solution)/shard_map/jit(_take)/gather | solution.py:33
  83.3 2.1 %select_bitcast_fusion.2 = bf16[96,4096]{0,1:T(8,128)(2,1)S(1)} fusion(bf16[4096,96]{1,0:T(8,128)(2,1)S(1)} %gather_fusion.5, pred[4096]{0:T(1024)(128)(4,1)S(1)} %compare_and_fusion.2), kind=kLoop, calls=%fused_computation.20 | loop fusion | flops 393216 | bytes 1576960 | tf_op jit(solution)/shard_map/jit(_take)/select_n | solution.py:33
  85.4 1.3 copy.79
  86.7 12.1 %gather_fusion.6 = bf16[4096,96]{1,0:T(8,128)(2,1)S(1)} fusion(bf16[96,4608]{0,1:T(8,128)(2,1)S(1)} %constant_dynamic-update-slice_fusion, s32[4096]{0:T(1024)S(1)} %get-tuple-element.26), kind=kCustom, calls=%fused_computation.6.clone | custom fusion | bytes 1589248 | tf_op jit(solution)/shard_map/jit(_take)/gather | solution.py:33
  98.8 2.1 %select_bitcast_fusion.1 = bf16[96,4096]{0,1:T(8,128)(2,1)S(1)} fusion(bf16[4096,96]{1,0:T(8,128)(2,1)S(1)} %gather_fusion.6, pred[4096]{0:T(1024)(128)(4,1)S(1)} %compare_and_fusion.1), kind=kLoop, calls=%fused_computation.19 | loop fusion | flops 393216 | bytes 1576960 | tf_op jit(solution)/shard_map/jit(_take)/select_n | solution.py:33
  101.0 1.3 copy.80
  102.3 12.1 %gather_fusion.7 = bf16[4096,96]{1,0:T(8,128)(2,1)S(1)} fusion(bf16[96,4608]{0,1:T(8,128)(2,1)S(1)} %constant_dynamic-update-slice_fusion, s32[4096]{0:T(1024)S(1)} %get-tuple-element.27), kind=kCustom, calls=%fused_computation.7.clone | custom fusion | bytes 1589248 | tf_op jit(solution)/shard_map/jit(_take)/gather | solution.py:33
  114.4 0.0 copy-start.1
  114.4 2.1 %select_bitcast_fusion = bf16[96,4096]{0,1:T(8,128)(2,1)S(1)} fusion(bf16[4096,96]{1,0:T(8,128)(2,1)S(1)} %gather_fusion.7, pred[4096]{0:T(1024)(128)(4,1)S(1)} %compare_and_fusion), kind=kLoop, calls=%fused_computation.18 | loop fusion | flops 393216 | bytes 1576960 | tf_op jit(solution)/shard_map/jit(_take)/select_n | solution.py:33
  116.6 0.5 copy.81
  117.1 0.0 copy-done.1
  117.1 1.6 pad_maximum_fusion
  118.7 0.2 copy.82
  118.9 14.5 %copy.83 = bf16[24,16,4096]{0,1,2:T(8,128)(2,1)} copy(bf16[24,16,4096]{2,1,0:T(8,128)(2,1)S(1)} %bitcast.62) | data formatting | bytes 6291456 | tf_op jit(solution)/shard_map/reshape | solution.py:36
  133.4 28.2 %fusion.18 = f32[4096,16,24]{2,1,0:T(8,128)} fusion(bf16[24,16,4096]{0,1,2:T(8,128)(2,1)} %copy.83, bf16[24,24,4096]{1,0,2:T(8,128)(2,1)} %copy.84), kind=kOutput, calls=%fused_computation.66 | convolution fusion | flops 75497472 | bytes 14155776 | tf_op jit(solution)/shard_map/imE,ijE->jmE/dot_general | solution.py:38
  161.6 20.3 %copy.85 = f32[4096,16,24]{0,1,2:T(8,128)} copy(f32[4096,16,24]{2,1,0:T(8,128)} %fusion.18) | data formatting | bytes 12582912 | tf_op jit(solution)/shard_map/imE,ijE->jmE/dot_general | solution.py:38
  181.9 3.6 %fusion.1 = f32[16,4096]{1,0:T(8,128)S(1)} fusion(f32[4096,16,24]{0,1,2:T(8,128)} %copy.85, bf16[6,4,16,4096]{3,2,1,0:T(8,128)(2,1)S(1)} %copy.82), kind=kLoop, calls=%fused_computation.11 | loop fusion | flops 4653056 | bytes 9699328 | tf_op jit(solution)/shard_map/reduce_sum | solution.py:41
  185.5 1.7 copy.91
  187.3 0.0 copy-start.5
  187.3 0.0 copy-start.7
  187.3 1.4 fusion.4
  188.7 0.1 reduce_sum.22
  188.8 0.0 copy-done.5
  188.8 2.2 %fusion.2 = f32[16,384]{1,0:T(8,128)S(1)} fusion(s32[4096]{0:T(1024)S(1)} %eq.15, f32[16,4096]{1,0:T(8,128)S(1)} %fusion.1, f32[16,4096]{1,0:T(8,128)S(1)} %reduce_sum.22, f32[4096]{0:T(1024)S(1)} %copy-done.5, f32[16]{0:T(128)S(1)} %copy-done.7), kind=kOutput, calls=%fused_computation.13 | convolution fusion | flops 303759360 | bytes 581696 | tf_op jit(solution)/shard_map/dot_general | solution.py:55
  191.0 1.9 collective-permute-start.4
  193.0 5.8 %collective-permute-start.5 = (f32[16,128]{1,0:T(8,128)S(1)}, f32[16,128]{1,0:T(8,128)S(1)}, u32[]{:S(2)}, u32[]{:S(2)}) collective-permute-start(f32[16,128]{1,0:T(8,128)S(1)} %get-tuple-element.17), channel_id=1, source_target_pairs={{4,0},{8,4},{12,8},{16,12},{20,16},{24,20},{28,24},{32,28},{36,32}... | collective-permute-start | bytes 24584 | tf_op jit(solution)/shard_map/ppermute | solution.py:16
  198.7 0.0 collective-permute-done.4
  198.7 1.3 collective-permute-done.5
  200.1 0.1 convolution_bitcast_fusion.1
  200.2 11.2 %psum.7 = f32[128]{0:T(128)} all-reduce(f32[128]{0:T(128)S(1)} %convolution_bitcast_fusion.1), channel_id=1, replica_groups=mesh['region'=64,'mode'=4] {'mode'}, use_global_device_ids=true, to_apply=%region_2.5 | all-reduce | flops 128 | bytes 1024 | tf_op jit(solution)/shard_map/psum | solution.py:60
  (23 shorter events, 0.2 us)
Async XLA Ops:
  0.6 199.4 %copy-start = (f32[16]{0:T(128)S(1)}, f32[16]{0:T(128)}, u32[]{:S(2)}) copy-start(f32[16]{0:T(128)} %param.21) | copy-start | bytes 196
  0.6 23.2 %copy-start.2 = (s32[4,4096]{1,0:T(4,128)S(1)}, s32[4,4096]{1,0:T(4,128)}, u32[]{:S(2)}) copy-start(s32[4,4096]{1,0:T(4,128)} %param.19) | copy-start | bytes 196612
  0.7 23.3 %copy-start.6 = (s32[128]{0:T(128)S(1)}, s32[128]{0:T(128)}, u32[]{:S(2)}) copy-start(s32[128]{0:T(128)} %param.20) | copy-start | bytes 1540
  3.9 51.5 %collective-permute-start = (bf16[96,128]{0,1:T(8,128)(2,1)S(1)}, bf16[96,128]{0,1:T(8,128)(2,1)S(1)}, u32[]{:S(2)}, u32[]{:S(2)}) collective-permute-start(bf16[96,128]{0,1:T(8,128)(2,1)S(1)} %select_bitcast_fusion.7), channel_id=1, source_target_pairs={{0,4},{4,8},{8,12},{12,16},{16,20},{20,24},{24,28},{28,32},{32,36}... | collective-permute-start | bytes 73736 | tf_op jit(solution)/shard_map/ppermute | solution.py:16
  6.7 48.8 %collective-permute-start.1 = (bf16[96,128]{0,1:T(8,128)(2,1)S(1)}, bf16[96,128]{0,1:T(8,128)(2,1)S(1)}, u32[]{:S(2)}, u32[]{:S(2)}) collective-permute-start(bf16[96,128]{0,1:T(8,128)(2,1)S(1)} %select_bitcast_fusion.6), channel_id=1, source_target_pairs={{4,0},{8,4},{12,8},{16,12},{20,16},{24,20},{28,24},{32,28},{36,32}... | collective-permute-start | bytes 73736 | tf_op jit(solution)/shard_map/ppermute | solution.py:16
  15.0 40.5 %collective-permute-start.2 = (bf16[96,128]{0,1:T(8,128)(2,1)S(1)}, bf16[96,128]{0,1:T(8,128)(2,1)S(1)}, u32[]{:S(2)}, u32[]{:S(2)}) collective-permute-start(bf16[96,128]{0,1:T(8,128)(2,1)S(1)} %select_bitcast_fusion.5), channel_id=1, source_target_pairs={{0,8},{4,12},{8,16},{12,20},{16,24},{20,28},{24,32},{28,36},{32,40... | collective-permute-start | bytes 73736 | tf_op jit(solution)/shard_map/ppermute | solution.py:16
  17.7 37.8 %collective-permute-start.3 = (bf16[96,128]{0,1:T(8,128)(2,1)S(1)}, bf16[96,128]{0,1:T(8,128)(2,1)S(1)}, u32[]{:S(2)}, u32[]{:S(2)}) collective-permute-start(bf16[96,128]{0,1:T(8,128)(2,1)S(1)} %select_bitcast_fusion.4), channel_id=1, source_target_pairs={{8,0},{12,4},{16,8},{20,12},{24,16},{28,20},{32,24},{36,28},{40,32... | collective-permute-start | bytes 73736 | tf_op jit(solution)/shard_map/ppermute | solution.py:16
  31.7 23.2 %copy-start.4 = (bf16[6,4,6,4]{2,3,1,0:T(4,128)(2,1)S(1)}, bf16[6,4,6,4]{2,3,1,0:T(4,128)(2,1)}, u32[]{:S(2)}) copy-start(bf16[6,4,6,4]{2,3,1,0:T(4,128)(2,1)} %param.15) | copy-start | bytes 3460
  114.4 2.7 %copy-start.1 = (bf16[96,4096]{1,0:T(8,128)(2,1)S(1)}, bf16[96,4096]{1,0:T(8,128)(2,1)}, u32[]{:S(2)}) copy-start(bf16[96,4096]{1,0:T(8,128)(2,1)} %copy.78) | copy-start | bytes 2359300
  187.3 1.5 copy-start.5
  187.3 1.5 copy-start.7
  191.0 7.7 %collective-permute-start.4 = (f32[16,128]{1,0:T(8,128)S(1)}, f32[16,128]{1,0:T(8,128)S(1)}, u32[]{:S(2)}, u32[]{:S(2)}) collective-permute-start(f32[16,128]{1,0:T(8,128)S(1)} %get-tuple-element.16), channel_id=1, source_target_pairs={{0,4},{4,8},{8,12},{12,16},{16,20},{20,24},{24,28},{28,32},{32,36}... | collective-permute-start | bytes 24584 | tf_op jit(solution)/shard_map/ppermute | solution.py:16
  193.0 7.1 %collective-permute-start.5 = (f32[16,128]{1,0:T(8,128)S(1)}, f32[16,128]{1,0:T(8,128)S(1)}, u32[]{:S(2)}, u32[]{:S(2)}) collective-permute-start(f32[16,128]{1,0:T(8,128)S(1)} %get-tuple-element.17), channel_id=1, source_target_pairs={{4,0},{8,4},{12,8},{16,12},{20,16},{24,20},{28,24},{32,28},{36,32}... | collective-permute-start | bytes 24584 | tf_op jit(solution)/shard_map/ppermute | solution.py:16
  200.1 11.4 %copy-start.3 = (f32[16,128]{1,0:T(8,128)}, f32[16,128]{1,0:T(8,128)S(1)}, u32[]{:S(2)}) copy-start(f32[16,128]{1,0:T(8,128)S(1)} %fusion.14) | copy-start | bytes 24580
where the time goes:
time: 213 us; the launch traced here: 211 us
  local copies, waits for them, and re-layouts  126 us (59%)
  matrix products  32 us (15%)
  starting transfers between devices  25 us (12%)
  other arithmetic  15 us (7%)
  blocking collectives  11.2 us (5%)
    gather x4, local copies, waits for them, and re-layouts, shards(): jnp.take(extended, connect[corner], axis=1).reshape(6, mode_dev, elem_count)  48.5 us
    reshape x2, local copies, waits for them, and re-layouts, shards(): stiff_flat = stiffness.reshape(24, 24, elem_count)  30.9 us
    dot_general x1, matrix products, shards(): jnp.einsum('imE,ijE->jmE', element_rows, stiff_flat, preferred_element_ty...  28.2 us
    ppermute x6, starting transfers between devices, shifted(): return lax.ppermute(array, axis, pairs)  25 us
    dot_general x1, local copies, waits for them, and re-layouts, shards(): jnp.einsum('imE,ijE->jmE', element_rows, stiff_flat, preferred_element_ty...  20.3 us
    reshape x1, local copies, waits for them, and re-layouts, shards(): jnp.stack(corner_rows, axis=1).reshape(24, mode_dev, elem_count)  14.5 us
    psum x1, blocking collectives, shards(): aggregate = lax.psum(weighted, 'mode')  11.2 us
    select_n x4, other arithmetic, shards(): jnp.take(extended, connect[corner], axis=1).reshape(6, mode_dev, elem_count)  8.59 us
  transfers between devices with their start and end apart: 6, of which 1 were waited for; matrix products, arithmetic and copies ran while one was open for 16% of the time, Pallas kernels for 0%

commit v1 on v0

v1 whole, which is shorter than its diff:
```python
import jax, jax.numpy as jnp
from jax import lax
from jax.experimental import pallas as pl
from jax.sharding import PartitionSpec as P
from jax.experimental.pallas import tpu as pltpu

NT = (((1,), (1,)), ((), ()))
SLOTS, VAR_DEV = 128, 128
f32, bf16 = jnp.float32, jnp.bfloat16


def split3(x):
    hi = x.astype(bf16)
    rest = x - hi.astype(f32)
    mid = rest.astype(bf16)
    low = (rest - mid.astype(f32)).astype(bf16)
    return jnp.concatenate([hi, mid, low], axis=0)


def fill_table(modes, table, tiles):
    def step(n, _):
        col = pl.ds(pl.multiple_of(n * 128, 128), 128)
        x = modes[:, col].astype(f32)
        x = jnp.concatenate([x, jnp.zeros((32, 128), f32)], axis=0)
        table[col, :] = x.T
        return 0
    lax.fori_loop(0, tiles, step, 0, unroll=2)


def send_kernel(modes, send_list, order, out0, out1, out2, out3, table):
    nodes = modes.shape[1]
    fill_table(modes, table, nodes // 128)
    for d, out in enumerate((out0, out1, out2, out3)):
        base = order[d] * SLOTS
        def step(s8, _):
            rows = [table[pl.ds(send_list[base + s8 * 16 + r], 1), :] for r in range(16)]
            out[pl.ds(pl.multiple_of(s8 * 16, 16), 16), :] = jnp.concatenate(rows, axis=0).astype(bf16)
            return 0
        lax.fori_loop(0, 8, step, 0)


PER = 8

def main_kernel(modes, ghost0, ghost1, ghost2, ghost3, order, stiff, weights, areas, lam, connect, var, own, near, far,
                table, gather_a, gather_b, f_buf, s_buf, u_buf, m_buf, *bufs):
    kbufs, ibufs, ksem, isem = bufs[:4], bufs[4:12], bufs[12], bufs[13]
    nodes = modes.shape[1]
    tiles = connect.shape[1] // 128
    gathers = (gather_a, gather_b)

    def k_copy(t, slot):
        return pltpu.make_async_copy(
            stiff.at[:, :, :, :, pl.ds(pl.multiple_of(t * 128, 128), 128)], kbufs[slot], ksem.at[slot])

    def i_copy(t, slot):
        return pltpu.make_async_copy(
            connect.at[:, pl.ds(pl.multiple_of(t * 128, 128), 128)], ibufs[slot], isem.at[slot])

    i_copy(0, PER - 1).start()
    for q in range(PER - 1):
        i_copy(q + 1, q).start()
    for q in range(4):
        k_copy(q, q).start()
    fill_table(modes, table, nodes // 128)
    for d, ghost in enumerate((ghost0, ghost1, ghost2, ghost3)):
        place = (order[d ^ 1]) * SLOTS
        table[pl.ds(pl.multiple_of(nodes + place, 128), SLOTS), :] = ghost[...].astype(f32)
    lane = lax.broadcasted_iota(jnp.int32, (128, 128), 1)
    row = lax.broadcasted_iota(jnp.int32, (128, 128), 0)
    eye = (lane == row).astype(bf16)[:96]
    summing = (row // 32 == lane).astype(bf16)

    def gather_rows(slot, dest):
        for e8 in range(0, 128, 8):
            for c in range(4):
                rows = [table[pl.ds(ibufs[slot][c, e8 + r], 1), :] for r in range(8)]
                dest[c, e8:e8 + 8, :] = jnp.concatenate(rows, axis=0)

    i_copy(0, PER - 1).wait()
    gather_rows(PER - 1, gather_a)
    i_copy(PER, PER - 1).start()

    def compute(t, kbuf, rows):
        for a in range(6):
            for c in range(4):
                for b in range(6):
                    first = ((a * 4 + c) * 6 + b) * 4
                    f_buf[first:first + 4, :] = kbuf[a, c, b].astype(f32)
        for i in range(24):
            for jb in range(i // 8, 3):
                s_buf[i * 24 + jb * 8:i * 24 + jb * 8 + 8, :] = (
                    f_buf[i * 24 + jb * 8:i * 24 + jb * 8 + 8, :] + f_buf[pl.ds(jb * 8 * 24 + i, 8, stride=24), :])
        g = [rows[c].astype(bf16) for c in range(4)]
        for c in range(4):
            u_buf[c] = lax.dot_general(eye, g[c], NT, preferred_element_type=f32)
        m_buf[...] = lax.dot_general(weights[...], jnp.concatenate(g, axis=1), NT, preferred_element_type=f32)
        out = []
        for h in range(2):
            u = [u_buf[c, k * 16 + h * 8:k * 16 + h * 8 + 8, :] for k in range(6) for c in range(4)]
            stiff_part = mass_part = None
            for i in range(24):
                acc = f_buf[i * 25:i * 25 + 1, :] * u[i]
                for j in range(i + 1, 24):
                    acc = acc + s_buf[i * 24 + j:i * 24 + j + 1, :] * u[j]
                stiff_part = acc * u[i] if stiff_part is None else stiff_part + acc * u[i]
                term = m_buf[i * 16 + h * 8:i * 16 + h * 8 + 8, :] * u[i]
                mass_part = term if mass_part is None else mass_part + term
            area = areas[pl.ds(t, 1), :]
            out.append(stiff_part - lam[h * 8:h * 8 + 8, :] * area * mass_part)
        energy = jnp.concatenate(out, axis=0)
        sums = jnp.dot(split3(energy), summing, preferred_element_type=f32)
        sums = sums[0:16] + sums[16:32] + sums[32:48]
        return pltpu.roll(sums, t * 4, 1)

    def body(it, blocks):
        for q in range(PER):
            t = it * PER + q
            i_copy(0, q).wait()
            k_copy(0, q % 4).wait()
            gather_rows(q, gathers[(q + 1) % 2])
            i_copy(jnp.minimum(t + PER + 1, tiles - 1), q).start()
            blocks = blocks + compute(t, kbufs[q % 4], gathers[q % 2])
            k_copy(jnp.minimum(t + 4, tiles - 1), q % 4).start()
        return blocks

    blocks = lax.fori_loop(0, tiles // PER, body, jnp.zeros((16, 128), f32))
    for q in range(PER):
        i_copy(0, q).wait()
    for q in range(4):
        k_copy(0, q).wait()
    table_t = (lax.broadcasted_iota(jnp.int32, (3 * VAR_DEV, 128), 0) == var[...]).astype(bf16)
    window = lax.dot_general(split3(blocks), table_t, NT, preferred_element_type=f32)
    window = window[0:16] + window[16:32] + window[32:48]
    for part, out in enumerate((own, near, far)):
        out[...] = window[:, part * VAR_DEV:(part + 1) * VAR_DEV]


VM = pl.BlockSpec(memory_space=pltpu.VMEM)
SM = pl.BlockSpec(memory_space=pltpu.SMEM)
HB = pl.BlockSpec(memory_space=pl.ANY)


def send_rows(modes, send_list, order):
    return pl.pallas_call(
        send_kernel,
        out_shape=[jax.ShapeDtypeStruct((SLOTS, 128), bf16)] * 4,
        in_specs=[VM, SM, SM], out_specs=(VM,) * 4,
        scratch_shapes=[pltpu.VMEM((modes.shape[1], 128), f32)],
        compiler_params=pltpu.CompilerParams(vmem_limit_bytes=16 * 2**20),
    )(modes, send_list, order)


def main_call(modes, ghosts, order, stiff, weights, areas, lam, connect, var):
    return pl.pallas_call(
        main_kernel,
        out_shape=[jax.ShapeDtypeStruct((16, VAR_DEV), f32)] * 3,
        in_specs=[VM, VM, VM, VM, VM, SM, HB, VM, VM, VM, HB, VM], out_specs=(VM,) * 3,
        scratch_shapes=[
            pltpu.VMEM((modes.shape[1] + 4 * SLOTS, 128), f32),
            pltpu.VMEM((4, 128, 128), f32), pltpu.VMEM((4, 128, 128), f32),
            pltpu.VMEM((576, 128), f32), pltpu.VMEM((576, 128), f32),
            pltpu.VMEM((4, 96, 128), f32), pltpu.VMEM((384, 128), f32),
            *[pltpu.VMEM((6, 4, 6, 4, 128), bf16)] * 4,
            *[pltpu.SMEM((4, 128), jnp.int32)] * PER,
            pltpu.SemaphoreType.DMA((4,)), pltpu.SemaphoreType.DMA((PER,)),
        ],
        compiler_params=pltpu.CompilerParams(vmem_limit_bytes=24 * 2**20),
    )(modes, *ghosts, order, stiff, weights, areas, lam, connect, var)


def mass_weights(mass_ref):
    m = mass_ref.reshape(24, 6, 4)
    eye = jnp.eye(16, dtype=mass_ref.dtype)
    w = jnp.einsum("ikc,mn->imckn", m, eye).reshape(384, 4, 96)
    return jnp.pad(w, ((0, 0), (0, 0), (0, 32))).reshape(384, 512)


OFFSETS = (1, -1, 2, -2)


def swap(array, axis, first):
    length = lax.axis_size(axis)
    pairs = []
    for i in range(first, length - 1, 2):
        pairs += [(i, i + 1), (i + 1, i)]
    return lax.ppermute(array, axis, pairs)


def swap_two(array, axis, first):
    length = lax.axis_size(axis)
    pairs = []
    for k in range(2 * first, length - 3, 4):
        for p in range(2):
            pairs += [(k + p, k + p + 2), (k + p + 2, k + p)]
    return lax.ppermute(array, axis, pairs)


def shards(
    modes, stiffness, mass_ref, areas, eigenvalues, send_list, connect, block_var, mode_weight
):
    region = lax.axis_index("region")
    mode_dev, node_count = modes.shape[1:]
    elem_count = connect.shape[1]
    flat = modes.reshape(6 * mode_dev, node_count)
    odd = region % 2
    upper = (region // 2) % 2
    order = jnp.stack([odd, 1 - odd, 2 + upper, 3 - upper]).astype(jnp.int32)
    sent = send_rows(flat, send_list.reshape(-1), order)
    received = [swap(sent[0], "region", 0), swap(sent[1], "region", 1),
                swap_two(sent[2], "region", 0), swap_two(sent[3], "region", 1)]
    step = block_var // VAR_DEV - region
    near = jnp.where(odd == 1, -1, 1)
    column = block_var % VAR_DEV + VAR_DEV * jnp.where(step == 0, 0, jnp.where(step == near, 1, 2))
    lam = jnp.broadcast_to(eigenvalues[:, None], (mode_dev, 128))
    own, sent_a, sent_b = main_call(
        flat, received, order, stiffness, mass_weights(mass_ref), areas.reshape(elem_count // 128, 128),
        lam, connect, column.reshape(1, 128))
    sens = own + swap(sent_a, "region", 0) + swap(sent_b, "region", 1)
    weighted = jnp.sum(mode_weight[:, None] * sens, axis=0)
    weighted = weighted + lax.ppermute(weighted, "mode", [(0, 1), (1, 0), (2, 3), (3, 2)])
    weighted = weighted + lax.ppermute(weighted, "mode", [(0, 3), (3, 0), (1, 2), (2, 1)])
    return (sens, weighted)


def solution(mesh):
    in_specs = (
        P(None, "mode", "region"),
        P(None, None, None, None, "region"),
        P(),
        P("region"),
        P("mode"),
        P(None, "region"),
        P(None, "region"),
        P("region"),
        P("mode"),
    )
    out_specs = (P("mode", "region"), P("region"))
    return jax.shard_map(shards, mesh=mesh, in_specs=in_specs, out_specs=out_specs, check_vma=False)
```

time: 213 us -> 74.6 us (0.35)
  local copies, waits for them, and re-layouts: 126 us -> 8.55 us
  Pallas kernels: 0 us -> 35.7 us
  matrix products: 32 us -> 0 us
  other arithmetic: 15 us -> 1.45 us
  blocking collectives: 11.2 us -> 0 us
  waiting for transfers between devices: 1.35 us -> 6.63 us
  starting transfers between devices: 25 us -> 21 us
    gather x8 -> x0, local copies, waits for them, and re-layouts: 51.3 us -> none  [the longest x4 48.5 us: shards(): jnp.take(extended, connect[corner], axis=1).reshape(6, mode_dev, elem_count)]
    reshape x5 -> x3, local copies, waits for them, and re-layouts: 47.1 us -> 3.31 us  [the longest x1 2.26 us: mass_weights(): w = jnp.einsum('ikc,mn->imckn', m, eye).reshape(384, 4, 96)]
    pallas_call x0 -> x2, Pallas kernels: none -> 35.7 us  [the longest x1 32.9 us: main_call(): pl.pallas_call(main_kernel, out_shape=[jax.ShapeDtypeStruct((16, VAR_DEV)...]
    dot_general x4 -> x0, matrix products: 32 us -> none  [the longest x1 28.2 us: shards(): jnp.einsum('imE,ijE->jmE', element_rows, stiff_flat, preferred_element_ty...]
    dot_general x1 -> x0, local copies, waits for them, and re-layouts: 20.3 us -> none  [shards(): jnp.einsum('imE,ijE->jmE', element_rows, stiff_flat, preferred_element_ty...]
    psum x1 -> x0, blocking collectives: 11.2 us -> none  [shards(): aggregate = lax.psum(weighted, 'mode')]
    select_n x8 -> x0, other arithmetic: 8.93 us -> none  [the longest x4 8.59 us: shards(): jnp.take(extended, connect[corner], axis=1).reshape(6, mode_dev, elem_count)]
    ppermute x6 -> x8, waiting for transfers between devices: 1.35 us -> 6.63 us  [the longest x4 2.93 us: swap(): return lax.ppermute(array, axis, pairs)]
  transfers between devices with their start and end apart: 6 -> 8, of which waited for: 1 -> 3; matrix products, arithmetic and copies ran while one was open for 16% -> 6% of each run, Pallas kernels for 0% -> 0%
where the time goes in v1:
time: 74.6 us; the launch traced here: 74.3 us
  Pallas kernels  35.7 us (48%)
  starting transfers between devices  21 us (28%)
  local copies, waits for them, and re-layouts  8.55 us (11%)
  waiting for transfers between devices  6.63 us (9%)
  other arithmetic  1.45 us (2%)
  between operations  0.89 us (1%)
    pallas_call x1, Pallas kernels, main_call(): pl.pallas_call(main_kernel, out_shape=[jax.ShapeDtypeStruct((16, VAR_DEV)...  32.9 us
    ppermute x4, starting transfers between devices, swap(): return lax.ppermute(array, axis, pairs)  12.4 us
    unnamed x18, local copies, waits for them, and re-layouts  4.18 us
    ppermute x2, starting transfers between devices, swap_two(): return lax.ppermute(array, axis, pairs)  3.99 us
    ppermute x1, starting transfers between devices, shards(): lax.ppermute(weighted, 'mode', [(0, 3), (3, 0), (1, 2), (2, 1)])  3.02 us
    ppermute x4, waiting for transfers between devices, swap(): return lax.ppermute(array, axis, pairs)  2.93 us
    pallas_call x1, Pallas kernels, send_rows(): pl.pallas_call(send_kernel, out_shape=[jax.ShapeDtypeStruct((SLOTS, 128),...  2.84 us
    reshape x1, local copies, waits for them, and re-layouts, mass_weights(): w = jnp.einsum('ikc,mn->imckn', m, eye).reshape(384, 4, 96)  2.26 us
  transfers between devices with their start and end apart: 8, of which 3 were waited for; matrix products, arithmetic and copies ran while one was open for 6% of the time, Pallas kernels for 0%

profile of v1, /device:TPU:6, one launch (start us, length us, event | category | flops | bytes accessed | tf_op | source)
XLA Modules:
  0.0 74.3 jit_solution(12488367335075050247)
XLA Ops:
  0.6 0.0 copy-start.8
  0.7 0.1 pad_add_fusion.order
  0.8 0.0 copy-start.1
  0.8 1.1 %copy-done.1 = bf16[6,16,4096]{2,1,0:T(8,128)(2,1)S(1)} copy-done((bf16[6,16,4096]{2,1,0:T(8,128)(2,1)S(1)}, bf16[6,16,4096]{2,1,0:T(8,128)(2,1)}, u32[]{:S(2)}) %copy-start.1) | copy-done | bytes 786456
  1.9 0.0 copy-start.5
  1.9 0.7 copy-done.5
  2.6 2.8 %shard_map.104 = (bf16[128,128]{1,0:T(8,128)(2,1)S(1)}, bf16[128,128]{1,0:T(8,128)(2,1)S(1)}, bf16[128,128]{1,0:T(8,128)(2,1)S(1)}, bf16[128,128]{1,0:T(8,128)(2,1)S(1)}) custom-call(bf16[96,4096]{1,0:T(8,128)(2,1)S(1)} %bitcast.17, s32[512]{0:T(512)S(1)} %bitcast.20, s32[4]{0:T(128)S(1)} %pad_add_fusion.order), custom_call_target="tpu_custom_call" | custom-call | tf_op jit(solution)/shard_map/pallas_call | solution.py:144
  5.4 0.1 collective-permute-start
  5.5 8.1 %collective-permute-start.1 = (bf16[128,128]{1,0:T(8,128)(2,1)S(1)}, bf16[128,128]{1,0:T(8,128)(2,1)S(1)}, u32[]{:S(2)}, u32[]{:S(2)}) collective-permute-start(bf16[128,128]{1,0:T(8,128)(2,1)S(1)} %get-tuple-element.10), channel_id=1, source_target_pairs={{4,8},{8,4},{12,16},{16,12},{20,24},{24,20},{28,32},{32,28},{36,40... | collective-permute-start | bytes 98312 | tf_op jit(solution)/shard_map/ppermute | solution.py:186
  13.6 0.1 collective-permute-start.2
  13.7 3.9 %collective-permute-start.3 = (bf16[128,128]{1,0:T(8,128)(2,1)S(1)}, bf16[128,128]{1,0:T(8,128)(2,1)S(1)}, u32[]{:S(2)}, u32[]{:S(2)}) collective-permute-start(bf16[128,128]{1,0:T(8,128)(2,1)S(1)} %get-tuple-element.12), channel_id=1, source_target_pairs={{8,16},{16,8},{12,20},{20,12},{24,32},{32,24},{28,36},{36,28},{40,... | collective-permute-start | bytes 98312 | tf_op jit(solution)/shard_map/ppermute | solution.py:195
  17.7 0.8 %copy.11 = bf16[24,6,4]{0,1,2:T(8,128)(2,1)S(1)} copy(bf16[24,6,4]{1,2,0:T(4,128)(2,1)} %bitcast.22) | data formatting | bytes 2304 | tf_op jit(solution)/shard_map/reshape | solution.py:172
  18.5 0.2 multiply_bitcast_fusion
  18.8 0.0 copy-done.8
  18.8 0.0 copy-start.7
  18.8 0.0 copy-start.2
  18.8 0.0 copy-start.3
  18.8 0.0 copy-start.4
  18.8 2.3 %reshape.30 = bf16[384,4,96]{0,2,1:T(8,128)(2,1)} reshape(bf16[24,16,4,6,16]{1,0,4,3,2:T(8,128)(2,1)S(1)} %multiply_bitcast_fusion) | data formatting | bytes 589824 | tf_op jit(solution)/shard_map/reshape | solution.py:174
  21.1 1.0 %pad.4 = bf16[384,4,128]{0,2,1:T(8,128)(2,1)S(1)} pad(bf16[384,4,96]{0,2,1:T(8,128)(2,1)} %reshape.30, bf16[]{:T(256)} %constant.65.clone.1), padding=0_0x0_0x0_32 | pad | bytes 688130 | tf_op jit(solution)/shard_map/jit(_pad)/pad | solution.py:175
  22.1 0.2 copy.13.weights
  22.3 0.0 collective-permute-done.ghost0
  22.3 0.0 collective-permute-done.1.ghost1
  22.3 0.0 collective-permute-done.2.ghost2
  22.3 0.0 collective-permute-done.3.ghost3
  22.3 0.0 copy-done.7
  22.4 0.1 broadcast_in_dim.10.lam
  22.4 0.0 copy-done.2
  22.4 0.0 copy-done.3
  22.4 0.0 copy-done.4
  22.4 0.0 copy-start
  22.5 2.3 %copy-done = bf16[6,4,6,4,4096]{4,3,2,1,0:T(4,128)(2,1)S(1)} copy-done((bf16[6,4,6,4,4096]{4,3,2,1,0:T(4,128)(2,1)S(1)}, bf16[6,4,6,4,4096]{4,3,2,1,0:T(4,128)(2,1)}, u32[]{:S(2)}) %copy-start) | copy-done | bytes 4718616
  24.8 0.0 copy-start.6
  24.8 32.9 %shard_map.105 = (f32[16,128]{1,0:T(8,128)S(1)}, f32[16,128]{1,0:T(8,128)S(1)}, f32[16,128]{1,0:T(8,128)S(1)}) custom-call(bf16[96,4096]{1,0:T(8,128)(2,1)S(1)} %bitcast.18, bf16[128,128]{1,0:T(8,128)(2,1)S(1)} %collective-permute-done.ghost0, bf16[128,128]{1,0:T(8,128)(2,1)S(1)} %collective-permute-done.1.ghost1, ...), custom_call_target="tpu_custom_call" | custom-call | tf_op jit(solution)/shard_map/pallas_call | solution.py:154
  57.7 0.1 collective-permute-start.4
  57.8 4.1 %collective-permute-start.5 = (f32[16,128]{1,0:T(8,128)S(1)}, f32[16,128]{1,0:T(8,128)S(1)}, u32[]{:S(2)}, u32[]{:S(2)}) collective-permute-start(f32[16,128]{1,0:T(8,128)S(1)} %get-tuple-element.15), channel_id=1, source_target_pairs={{4,8},{8,4},{12,16},{16,12},{20,24},{24,20},{28,32},{32,28},{36,40... | collective-permute-start | bytes 24584 | tf_op jit(solution)/shard_map/ppermute | solution.py:186
  61.9 0.0 collective-permute-done.4
  61.9 2.9 %collective-permute-done.5 = f32[16,128]{1,0:T(8,128)S(1)} collective-permute-done((f32[16,128]{1,0:T(8,128)S(1)}, f32[16,128]{1,0:T(8,128)S(1)}, u32[]{:S(2)}, u32[]{:S(2)}) %collective-permute-start.5) | collective-permute-done | bytes 8224 | tf_op jit(solution)/shard_map/ppermute | solution.py:186
  64.9 0.0 copy-done.6
  64.9 0.6 multiply_reduce_fusion
  65.5 1.6 %collective-permute-start.6 = (f32[128]{0:T(128)S(1)}, f32[128]{0:T(128)S(1)}, u32[]{:S(2)}, u32[]{:S(2)}) collective-permute-start(f32[128]{0:T(128)S(1)} %get-tuple-element.16), channel_id=1, source_target_pairs={{0,1},{1,0},{2,3},{3,2},{4,5},{5,4},{6,7},{7,6},{8,9},{9,8},{10,11... | collective-permute-start | bytes 1544 | tf_op jit(solution)/shard_map/ppermute | solution.py:220
  67.1 2.0 %collective-permute-done.6 = f32[128]{0:T(128)S(1)} collective-permute-done((f32[128]{0:T(128)S(1)}, f32[128]{0:T(128)S(1)}, u32[]{:S(2)}, u32[]{:S(2)}) %collective-permute-start.6) | collective-permute-done | bytes 544 | tf_op jit(solution)/shard_map/ppermute | solution.py:220
  69.0 3.0 %collective-permute-start.7 = (f32[128]{0:T(128)S(1)}, f32[128]{0:T(128)S(1)}, u32[]{:S(2)}, u32[]{:S(2)}) collective-permute-start(f32[128]{0:T(128)S(1)} %add.42), channel_id=1, source_target_pairs={{0,3},{3,0},{1,2},{2,1},{4,7},{7,4},{5,6},{6,5},{8,11},{11,8},{9,1... | collective-permute-start | bytes 1544 | tf_op jit(solution)/shard_map/ppermute | solution.py:221
  72.0 1.7 %collective-permute-done.7 = f32[128]{0:T(128)S(1)} collective-permute-done((f32[128]{0:T(128)S(1)}, f32[128]{0:T(128)S(1)}, u32[]{:S(2)}, u32[]{:S(2)}) %collective-permute-start.7) | collective-permute-done | bytes 544 | tf_op jit(solution)/shard_map/ppermute | solution.py:221
  73.8 0.5 add.43
  (3 shorter events, 0.0 us)
Async XLA Ops:
  0.6 18.1 %copy-start.8 = (s32[128]{0:T(128)S(1)}, s32[128]{0:T(128)}, u32[]{:S(2)}) copy-start(s32[128]{0:T(128)} %param.16) | copy-start | bytes 1540
  0.8 1.1 %copy-start.1 = (bf16[6,16,4096]{2,1,0:T(8,128)(2,1)S(1)}, bf16[6,16,4096]{2,1,0:T(8,128)(2,1)}, u32[]{:S(2)}) copy-start(bf16[6,16,4096]{2,1,0:T(8,128)(2,1)} %param.9) | copy-start | bytes 2359300
  1.9 0.7 copy-start.5
  5.4 16.9 %collective-permute-start = (bf16[128,128]{1,0:T(8,128)(2,1)S(1)}, bf16[128,128]{1,0:T(8,128)(2,1)S(1)}, u32[]{:S(2)}, u32[]{:S(2)}) collective-permute-start(bf16[128,128]{1,0:T(8,128)(2,1)S(1)} %get-tuple-element.9), channel_id=1, source_target_pairs={{0,4},{4,0},{8,12},{12,8},{16,20},{20,16},{24,28},{28,24},{32,36},... | collective-permute-start | bytes 98312 | tf_op jit(solution)/shard_map/ppermute | solution.py:186
  5.5 16.8 %collective-permute-start.1 = (bf16[128,128]{1,0:T(8,128)(2,1)S(1)}, bf16[128,128]{1,0:T(8,128)(2,1)S(1)}, u32[]{:S(2)}, u32[]{:S(2)}) collective-permute-start(bf16[128,128]{1,0:T(8,128)(2,1)S(1)} %get-tuple-element.10), channel_id=1, source_target_pairs={{4,8},{8,4},{12,16},{16,12},{20,24},{24,20},{28,32},{32,28},{36,40... | collective-permute-start | bytes 98312 | tf_op jit(solution)/shard_map/ppermute | solution.py:186
  13.6 8.7 %collective-permute-start.2 = (bf16[128,128]{1,0:T(8,128)(2,1)S(1)}, bf16[128,128]{1,0:T(8,128)(2,1)S(1)}, u32[]{:S(2)}, u32[]{:S(2)}) collective-permute-start(bf16[128,128]{1,0:T(8,128)(2,1)S(1)} %get-tuple-element.11), channel_id=1, source_target_pairs={{0,8},{8,0},{4,12},{12,4},{16,24},{24,16},{20,28},{28,20},{32,40},... | collective-permute-start | bytes 98312 | tf_op jit(solution)/shard_map/ppermute | solution.py:195
  13.7 8.6 %collective-permute-start.3 = (bf16[128,128]{1,0:T(8,128)(2,1)S(1)}, bf16[128,128]{1,0:T(8,128)(2,1)S(1)}, u32[]{:S(2)}, u32[]{:S(2)}) collective-permute-start(bf16[128,128]{1,0:T(8,128)(2,1)S(1)} %get-tuple-element.12), channel_id=1, source_target_pairs={{8,16},{16,8},{12,20},{20,12},{24,32},{32,24},{28,36},{36,28},{40,... | collective-permute-start | bytes 98312 | tf_op jit(solution)/shard_map/ppermute | solution.py:195
  18.8 3.6 %copy-start.7 = (f32[16]{0:T(128)S(1)}, f32[16]{0:T(128)}, u32[]{:S(2)}) copy-start(f32[16]{0:T(128)} %param.13) | copy-start | bytes 196
  18.8 3.7 %copy-start.2 = (bf16[6,16,4096]{2,1,0:T(8,128)(2,1)S(1)}, bf16[6,16,4096]{2,1,0:T(8,128)(2,1)}, u32[]{:S(2)}) copy-start(bf16[6,16,4096]{2,1,0:T(8,128)(2,1)} %param.9) | copy-start | bytes 2359300
  18.8 3.6 %copy-start.3 = (s32[4,4096]{1,0:T(4,128)S(1)}, s32[4,4096]{1,0:T(4,128)}, u32[]{:S(2)}) copy-start(s32[4,4096]{1,0:T(4,128)} %connect.1) | copy-start | bytes 196612
  18.8 3.6 %copy-start.4 = (f32[4096]{0:T(1024)S(1)}, f32[4096]{0:T(1024)}, u32[]{:S(2)}) copy-start(f32[4096]{0:T(1024)} %param.12) | copy-start | bytes 49156
  22.4 2.3 %copy-start = (bf16[6,4,6,4,4096]{4,3,2,1,0:T(4,128)(2,1)S(1)}, bf16[6,4,6,4,4096]{4,3,2,1,0:T(4,128)(2,1)}, u32[]{:S(2)}) copy-start(bf16[6,4,6,4,4096]{4,3,2,1,0:T(4,128)(2,1)} %stiff.1) | copy-start | bytes 14155780
  24.8 40.1 %copy-start.6 = (f32[16]{0:T(128)S(1)}, f32[16]{0:T(128)}, u32[]{:S(2)}) copy-start(f32[16]{0:T(128)} %param.17) | copy-start | bytes 196
  57.7 4.2 %collective-permute-start.4 = (f32[16,128]{1,0:T(8,128)S(1)}, f32[16,128]{1,0:T(8,128)S(1)}, u32[]{:S(2)}, u32[]{:S(2)}) collective-permute-start(f32[16,128]{1,0:T(8,128)S(1)} %get-tuple-element.14), channel_id=1, source_target_pairs={{0,4},{4,0},{8,12},{12,8},{16,20},{20,16},{24,28},{28,24},{32,36},... | collective-permute-start | bytes 24584 | tf_op jit(solution)/shard_map/ppermute | solution.py:186
  57.8 7.1 %collective-permute-start.5 = (f32[16,128]{1,0:T(8,128)S(1)}, f32[16,128]{1,0:T(8,128)S(1)}, u32[]{:S(2)}, u32[]{:S(2)}) collective-permute-start(f32[16,128]{1,0:T(8,128)S(1)} %get-tuple-element.15), channel_id=1, source_target_pairs={{4,8},{8,4},{12,16},{16,12},{20,24},{24,20},{28,32},{32,28},{36,40... | collective-permute-start | bytes 24584 | tf_op jit(solution)/shard_map/ppermute | solution.py:186
  65.5 3.5 %collective-permute-start.6 = (f32[128]{0:T(128)S(1)}, f32[128]{0:T(128)S(1)}, u32[]{:S(2)}, u32[]{:S(2)}) collective-permute-start(f32[128]{0:T(128)S(1)} %get-tuple-element.16), channel_id=1, source_target_pairs={{0,1},{1,0},{2,3},{3,2},{4,5},{5,4},{6,7},{7,6},{8,9},{9,8},{10,11... | collective-permute-start | bytes 1544 | tf_op jit(solution)/shard_map/ppermute | solution.py:220
  69.0 4.8 %collective-permute-start.7 = (f32[128]{0:T(128)S(1)}, f32[128]{0:T(128)S(1)}, u32[]{:S(2)}, u32[]{:S(2)}) collective-permute-start(f32[128]{0:T(128)S(1)} %add.42), channel_id=1, source_target_pairs={{0,3},{3,0},{1,2},{2,1},{4,7},{7,4},{5,6},{6,5},{8,11},{11,8},{9,1... | collective-permute-start | bytes 1544 | tf_op jit(solution)/shard_map/ppermute | solution.py:221

commit v2 on v0

v2 whole, which is shorter than its diff:
```python
import jax
import jax.numpy as jnp
from jax import lax
from jax.experimental import pallas as pl
from jax.experimental.pallas import tpu as pltpu
from jax.sharding import PartitionSpec as P

NT = (((1,), (1,)), ((), ()))
SLOTS, VAR_DEV = 128, 128
TILE, CHUNK = 128, 512
TILES = CHUNK // TILE
BESIDE = 0
f32, bf16 = jnp.float32, jnp.bfloat16


def iota(shape, dim):
    return lax.broadcasted_iota(jnp.int32, shape, dim)


def pieces(x):
    hi = x.astype(bf16)
    rest = x - hi.astype(f32)
    mid = rest.astype(bf16)
    low = (rest - mid.astype(f32)).astype(bf16)
    return jnp.concatenate([hi, mid, low], axis=0)


def mass_matrix(mass, stage, weights):
    stage[...] = jnp.zeros_like(stage)
    for a in range(6):
        for c in range(4):
            first = (a * 4 + c) * 4
            stage[first:first + 4, 0:6] = mass[a, c].astype(f32)
    values = stage[...].astype(bf16)
    col = iota((512, 96), 0)
    comp, corner = (col % 128) // 16, col // 128
    spread = (iota((128, 128), 0) // 16 == iota((128, 128), 1)).astype(bf16)
    same = iota((128, 512), 0) % 16 == iota((128, 512), 1) % 16
    for d in range(4):
        pick = ((comp < 6) & (iota((512, 96), 1) == (comp * 4 + corner) * 4 + d)).astype(bf16)
        by_col = jnp.dot(pick, values, preferred_element_type=f32).astype(bf16)
        block = lax.dot_general(spread, by_col, NT, preferred_element_type=f32)
        weights[d * 128:d * 128 + 128, :] = jnp.where(same, block, 0.0).astype(bf16)


def send_kernel(modes, send_list, order, mass, out0, out1, out2, out3, table, weights,
                near, lists, stage, sem, list_sem):
    nodes = modes.shape[1]
    width = nodes // 4

    def copy(n):
        return pltpu.make_async_copy(modes.at[:, pl.ds(n * width, width)], near.at[:, pl.ds(n * width, width)], sem.at[n])

    for n in range(4):
        copy(n).start()
    list_copy = pltpu.make_async_copy(send_list, lists, list_sem)
    list_copy.start()
    mass_matrix(mass, stage, weights)
    for n in range(4):
        copy(n).wait()

        def transpose(q, _):
            col = pl.ds(pl.multiple_of(n * width + q * TILE, TILE), TILE)
            x = jnp.concatenate([near[:, col].astype(f32), jnp.zeros((32, TILE), f32)], axis=0)
            table[col, :] = x.T
            return 0

        lax.fori_loop(0, width // TILE, transpose, 0, unroll=4)
    list_copy.wait()
    for d, out in enumerate((out0, out1, out2, out3)):
        which = order[d]

        def rows16(s, _):
            rows = [table[pl.ds(lists[which, s * 16 + r], 1), :] for r in range(16)]
            out[pl.ds(pl.multiple_of(s * 16, 16), 16), :] = jnp.concatenate(rows, axis=0).astype(bf16)
            return 0

        lax.fori_loop(0, SLOTS // 16, rows16, 0, unroll=2)


def main_kernel(table_in, ghost0, ghost1, ghost2, ghost3, order, stiff, weights, areas, lam, connect, var,
                own, near, far, table, gather_a, gather_b, f_bufs, s_bufs, u_bufs, mass_rows, masses,
                index_a, index_b, stiff_near, energies, blocks, stiff_sem, index_sem):
    nodes = table_in.shape[0]
    chunks = connect.shape[1] // CHUNK
    gathers, indices = (gather_a, gather_b), (index_a, index_b)

    def stiff_copy(n):
        return pltpu.make_async_copy(
            stiff.at[:, :, :, :, pl.ds(pl.multiple_of(n * TILE, TILE), TILE)], stiff_near.at[n], stiff_sem.at[n])

    def index_copy(n, slot):
        n = jnp.minimum(n, chunks - 1)
        return pltpu.make_async_copy(
            connect.at[:, pl.ds(pl.multiple_of(n * CHUNK, CHUNK), CHUNK)], indices[slot], index_sem.at[slot])

    index_copy(0, 0).start()
    index_copy(1, 1).start()
    for n in range(chunks * TILES):
        stiff_copy(n).start()
    table[0:nodes, :] = table_in[...]
    for d, ghost in enumerate((ghost0, ghost1, ghost2, ghost3)):
        place = pl.multiple_of(nodes + order[d ^ 1] * SLOTS, SLOTS)
        table[pl.ds(place, SLOTS), :] = ghost[...].astype(f32)
    summing = (iota((TILE, TILE), 0) // 32 == iota((TILE, TILE), 1)).astype(bf16)

    def gather_rows(slot, first, last, start=0):
        index, dest = indices[slot], gathers[slot]
        for e in range(first, last):
            for c in range(4):
                dest[c, pl.ds(start + e, 1), :] = table[pl.ds(index[c, start + e], 1), :]

    index_copy(0, 0).wait()
    gather_rows(0, 0, CHUNK)
    index_copy(2, 0).start()

    def prepare(n, q, slot):
        rows, f_buf, s_buf = gathers[slot], f_bufs.at[q], s_bufs.at[q]
        near = stiff_near.at[n * TILES + q].reshape(576, TILE)
        part = slice(q * TILE, (q + 1) * TILE)
        mass = None
        for c in range(4):
            values = rows[c, part, :]
            u_bufs[q, c] = values.T
            term = mass_rows[part, c * 128:(c + 1) * 128] * values
            mass = term if mass is None else mass + term
        mass = mass.T
        masses[q] = sum(mass[k * 16:k * 16 + 16, :] for k in range(1, 6)) + mass[0:16, :]
        for i in range(0, 576, 16):
            f_buf[i:i + 16, :] = near[i:i + 16, :].astype(f32)
        for i in range(24):
            for j in range(i // 8 * 8, 24, 8):
                s_buf[i * 24 + j:i * 24 + j + 8, :] = (
                    f_buf[i * 24 + j:i * 24 + j + 8, :] + f_buf[pl.ds(j * 24 + i, 8, stride=24), :])

    def tile_energy(n, q):
        f_buf, s_buf, u_buf = f_bufs.at[q], s_bufs.at[q], u_bufs.at[q]
        halves = []
        for h in range(2):
            u = [u_buf[c, k * 16 + h * 8:k * 16 + h * 8 + 8, :] for k in range(6) for c in range(4)]
            total = None
            for i in range(24):
                acc = f_buf[i * 25:i * 25 + 1, :] * u[i]
                for j in range(i + 1, 24):
                    acc = acc + s_buf[i * 24 + j:i * 24 + j + 1, :] * u[j]
                total = acc * u[i] if total is None else total + acc * u[i]
            halves.append(total)
        area = areas[pl.ds(n * TILES + q, 1), :]
        energies[n, q] = jnp.concatenate(halves, axis=0) - lam[...] * area * masses[q]

    def add_blocks(n):
        values = jnp.concatenate([pieces(energies[n, q]) for q in range(TILES)], axis=0)
        sums = jnp.dot(values, summing, preferred_element_type=f32)
        for q in range(TILES):
            one = sums[q * 48:q * 48 + 16] + sums[q * 48 + 16:q * 48 + 32] + sums[q * 48 + 32:q * 48 + 48]
            blocks[...] += pltpu.roll(one, n * (CHUNK // 32) + q * 4, 1)

    def body(it, _):
        for slot in range(2):
            n = it * 2 + slot
            index_copy(0, 1 - slot).wait()
            for q in range(TILES):
                stiff_copy(n * TILES + q).wait()

            gather_rows(1 - slot, 0, CHUNK - TILES * BESIDE)
            rows = jnp.concatenate([gathers[slot][c].astype(bf16) for c in range(4)], axis=1)
            mass_rows[...] = jnp.dot(rows, weights[...], preferred_element_type=f32)
            add_blocks((n + chunks - 1) % chunks)
            for q in range(TILES):
                prepare(n, q, slot)

            def one_tile(q, _, n=n, slot=slot):
                tile_energy(n, q)
                if BESIDE:
                    gather_rows(1 - slot, 0, BESIDE, CHUNK - TILES * BESIDE + q * BESIDE)
                return 0

            lax.fori_loop(0, TILES, one_tile, 0)
            index_copy(n + 3, 1 - slot).start()
        return 0

    energies[...] = jnp.zeros_like(energies)
    blocks[...] = jnp.zeros_like(blocks)
    lax.fori_loop(0, chunks // 2, body, 0)
    add_blocks(chunks - 1)
    for slot in range(2):
        index_copy(0, slot).wait()
    columns = (iota((3 * VAR_DEV, 128), 0) == var[...]).astype(bf16)
    window = lax.dot_general(pieces(blocks[...]), columns, NT, preferred_element_type=f32)
    window = window[0:16] + window[16:32] + window[32:48]
    for part, out in enumerate((own, near, far)):
        out[...] = window[:, part * VAR_DEV:(part + 1) * VAR_DEV]


VM = pl.BlockSpec(memory_space=pltpu.VMEM)
SM = pl.BlockSpec(memory_space=pltpu.SMEM)
HB = pl.BlockSpec(memory_space=pltpu.HBM)


def send_rows(modes, send_list, order, mass_ref):
    nodes = modes.shape[1]
    return pl.pallas_call(
        send_kernel,
        out_shape=[jax.ShapeDtypeStruct((SLOTS, 128), bf16)] * 4
        + [jax.ShapeDtypeStruct((nodes, 128), f32), jax.ShapeDtypeStruct((512, 512), bf16)],
        in_specs=[HB, HB, SM, VM], out_specs=[VM] * 6,
        scratch_shapes=[
            pltpu.VMEM(modes.shape, bf16), pltpu.SMEM(send_list.shape, jnp.int32), pltpu.VMEM((96, 128), f32),
            pltpu.SemaphoreType.DMA((4,)), pltpu.SemaphoreType.DMA,
        ],
        compiler_params=pltpu.CompilerParams(vmem_limit_bytes=12 * 2**20),
    )(modes, send_list, order, mass_ref.transpose(0, 1, 3, 2))


def main_call(table, ghosts, order, stiff, weights, areas, lam, connect, var):
    chunks = connect.shape[1] // CHUNK
    return pl.pallas_call(
        main_kernel,
        out_shape=[jax.ShapeDtypeStruct((16, VAR_DEV), f32)] * 3,
        in_specs=[VM, VM, VM, VM, VM, SM, HB, VM, VM, VM, HB, VM], out_specs=[VM] * 3,
        scratch_shapes=[
            pltpu.VMEM((table.shape[0] + 4 * SLOTS, 128), f32),
            pltpu.VMEM((4, CHUNK, 128), f32), pltpu.VMEM((4, CHUNK, 128), f32),
            pltpu.VMEM((TILES, 576, 128), f32), pltpu.VMEM((TILES, 576, 128), f32),
            pltpu.VMEM((TILES, 4, 128, 128), f32), pltpu.VMEM((CHUNK, 512), f32), pltpu.VMEM((TILES, 16, 128), f32),
            pltpu.SMEM((4, CHUNK), jnp.int32), pltpu.SMEM((4, CHUNK), jnp.int32),
            pltpu.VMEM((chunks * TILES, 6, 4, 6, 4, TILE), bf16),
            pltpu.VMEM((chunks, TILES, 16, 128), f32), pltpu.VMEM((16, 128), f32),
            pltpu.SemaphoreType.DMA((chunks * TILES,)), pltpu.SemaphoreType.DMA((2,)),
        ],
        compiler_params=pltpu.CompilerParams(vmem_limit_bytes=57 * 2**20),
    )(table, *ghosts, order, stiff, weights, areas, lam, connect, var)


OFFSETS = (1, -1, 2, -2)


def swap(array, axis, first):
    length = lax.axis_size(axis)
    pairs = []
    for i in range(first, length - 1, 2):
        pairs += [(i, i + 1), (i + 1, i)]
    return lax.ppermute(array, axis, pairs)


def swap_two(array, axis, first):
    length = lax.axis_size(axis)
    pairs = []
    for k in range(2 * first, length - 3, 4):
        for p in range(2):
            pairs += [(k + p, k + p + 2), (k + p + 2, k + p)]
    return lax.ppermute(array, axis, pairs)


def shards(
    modes, stiffness, mass_ref, areas, eigenvalues, send_list, connect, block_var, mode_weight
):
    region = lax.axis_index("region")
    mode_dev, node_count = modes.shape[1:]
    elem_count = connect.shape[1]
    flat = modes.reshape(6 * mode_dev, node_count)
    odd = region % 2
    upper = (region // 2) % 2
    order = jnp.stack([odd, 1 - odd, 2 + upper, 3 - upper]).astype(jnp.int32)
    *sent, table, weights = send_rows(flat, send_list, order, mass_ref)
    received = [swap(sent[0], "region", 0), swap(sent[1], "region", 1),
                swap_two(sent[2], "region", 0), swap_two(sent[3], "region", 1)]
    step = block_var // VAR_DEV - region
    near = jnp.where(odd == 1, -1, 1)
    column = block_var % VAR_DEV + VAR_DEV * jnp.where(step == 0, 0, jnp.where(step == near, 1, 2))
    lam = jnp.broadcast_to(eigenvalues[:, None], (mode_dev, 128))
    own, sent_a, sent_b = main_call(
        table, received, order, stiffness, weights, areas.reshape(elem_count // 128, 128),
        lam, connect, column.reshape(1, 128))
    sens = own + swap(sent_a, "region", 0) + swap(sent_b, "region", 1)
    weighted = jnp.sum(mode_weight[:, None] * sens, axis=0)
    other = [lax.ppermute(weighted, "mode", [(q, q ^ by) for q in range(4)]) for by in (1, 2, 3)]
    weighted = (weighted + other[0]) + (other[1] + other[2])
    return (sens, weighted)


def solution(mesh):
    in_specs = (
        P(None, "mode", "region"),
        P(None, None, None, None, "region"),
        P(),
        P("region"),
        P("mode"),
        P(None, "region"),
        P(None, "region"),
        P("region"),
        P("mode"),
    )
    out_specs = (P("mode", "region"), P("region"))
    return jax.shard_map(shards, mesh=mesh, in_specs=in_specs, out_specs=out_specs, check_vma=False)
```

time: 213 us -> 71 us (0.33)
  local copies, waits for them, and re-layouts: 126 us -> 6.04 us
  matrix products: 32 us -> 0 us
  Pallas kernels: 0 us -> 29.2 us
  other arithmetic: 15 us -> 3.04 us
  blocking collectives: 11.2 us -> 0 us
  waiting for transfers between devices: 1.35 us -> 10.7 us
  starting transfers between devices: 25 us -> 20.9 us
    gather x8 -> x0, local copies, waits for them, and re-layouts: 51.3 us -> none  [the longest x4 48.5 us: shards(): jnp.take(extended, connect[corner], axis=1).reshape(6, mode_dev, elem_count)]
    reshape x5 -> x0, local copies, waits for them, and re-layouts: 47.1 us -> none  [the longest x2 30.9 us: shards(): stiff_flat = stiffness.reshape(24, 24, elem_count)]
    dot_general x4 -> x0, matrix products: 32 us -> none  [the longest x1 28.2 us: shards(): jnp.einsum('imE,ijE->jmE', element_rows, stiff_flat, preferred_element_ty...]
    pallas_call x0 -> x2, Pallas kernels: none -> 29.2 us  [the longest x1 25.8 us: main_call(): pl.pallas_call(main_kernel, out_shape=[jax.ShapeDtypeStruct((16, VAR_DEV)...]
    dot_general x1 -> x0, local copies, waits for them, and re-layouts: 20.3 us -> none  [shards(): jnp.einsum('imE,ijE->jmE', element_rows, stiff_flat, preferred_element_ty...]
    psum x1 -> x0, blocking collectives: 11.2 us -> none  [shards(): aggregate = lax.psum(weighted, 'mode')]
    ppermute x6 -> x9, waiting for transfers between devices: 1.35 us -> 10.7 us  [the longest x3 4.55 us: shards(): lax.ppermute(weighted, 'mode', [(q, q ^ by) for q in range(4)])]
    select_n x8 -> x0, other arithmetic: 8.93 us -> none  [the longest x4 8.59 us: shards(): jnp.take(extended, connect[corner], axis=1).reshape(6, mode_dev, elem_count)]
  transfers between devices with their start and end apart: 6 -> 9, of which waited for: 1 -> 4; matrix products, arithmetic and copies ran while one was open for 16% -> 2% of each run, Pallas kernels for 0% -> 0%
where the time goes in v2:
time: 71 us; the launch traced here: 70.6 us
  Pallas kernels  29.2 us (41%)
  starting transfers between devices  20.9 us (29%)
  waiting for transfers between devices  10.7 us (15%)
  local copies, waits for them, and re-layouts  6.04 us (9%)
  other arithmetic  3.04 us (4%)
  between operations  0.81 us (1%)
    pallas_call x1, Pallas kernels, main_call(): pl.pallas_call(main_kernel, out_shape=[jax.ShapeDtypeStruct((16, VAR_DEV)...  25.8 us
    ppermute x4, starting transfers between devices, swap(): return lax.ppermute(array, axis, pairs)  12.2 us
    unnamed x22, local copies, waits for them, and re-layouts  4.7 us
    ppermute x3, starting transfers between devices, shards(): lax.ppermute(weighted, 'mode', [(q, q ^ by) for q in range(4)])  4.7 us
    ppermute x3, waiting for transfers between devices, shards(): lax.ppermute(weighted, 'mode', [(q, q ^ by) for q in range(4)])  4.55 us
    ppermute x2, starting transfers between devices, swap_two(): return lax.ppermute(array, axis, pairs)  3.99 us
    pallas_call x1, Pallas kernels, send_rows(): pl.pallas_call(send_kernel, out_shape=[jax.ShapeDtypeStruct((SLOTS, 128),...  3.39 us
    ppermute x4, waiting for transfers between devices, swap(): return lax.ppermute(array, axis, pairs)  3.3 us
  transfers between devices with their start and end apart: 9, of which 4 were waited for; matrix products, arithmetic and copies ran while one was open for 2% of the time, Pallas kernels for 0%

profile of v2, /device:TPU:6, one launch (start us, length us, event | category | flops | bytes accessed | tf_op | source)
XLA Modules:
  0.0 70.6 jit_solution(13243068069244921031)
XLA Ops:
  0.6 0.0 copy-start.10
  0.7 0.1 pad_add_fusion.order
  0.8 0.0 copy-start.4
  0.8 0.0 copy-start.1
  0.8 1.1 %copy-done.1 = bf16[6,16,4096]{2,1,0:T(8,128)(2,1)S(1)} copy-done((bf16[6,16,4096]{2,1,0:T(8,128)(2,1)S(1)}, bf16[6,16,4096]{2,1,0:T(8,128)(2,1)}, u32[]{:S(2)}) %copy-start.1) | copy-done | bytes 786456
  1.9 0.0 copy-start.3
  1.9 0.7 %copy-done.3 = bf16[6,4,6,4]{2,3,1,0:T(4,128)(2,1)S(1)} copy-done((bf16[6,4,6,4]{2,3,1,0:T(4,128)(2,1)S(1)}, bf16[6,4,6,4]{2,3,1,0:T(4,128)(2,1)}, u32[]{:S(2)}) %copy-start.3) | copy-done | bytes 1176
  2.6 0.0 copy-start.5
  2.6 0.7 copy-done.5
  3.3 3.4 %shard_map.104 = (bf16[128,128]{1,0:T(8,128)(2,1)S(1)}, bf16[128,128]{1,0:T(8,128)(2,1)S(1)}, bf16[128,128]{1,0:T(8,128)(2,1)S(1)}, bf16[128,128]{1,0:T(8,128)(2...) custom-call(bf16[96,4096]{1,0:T(8,128)(2,1)S(1)} %bitcast.9, s32[4,128]{1,0:T(4,128)S(1)} %copy-done.5, ...), custom_call_target="tpu_custom_call" | custom-call | tf_op jit(solution)/shard_map/pallas_call | solution.py:202
  6.7 0.0 copy-start
  6.7 1.3 %copy-done = f32[4096,128]{1,0:T(8,128)} copy-done((f32[4096,128]{1,0:T(8,128)}, f32[4096,128]{1,0:T(8,128)S(1)}, u32[]{:S(2)}) %copy-start) | copy-done | bytes 2097176
  8.1 0.0 copy-start.2
  8.1 0.8 %copy-done.2 = bf16[512,512]{1,0:T(8,128)(2,1)} copy-done((bf16[512,512]{1,0:T(8,128)(2,1)}, bf16[512,512]{1,0:T(8,128)(2,1)S(1)}, u32[]{:S(2)}) %copy-start.2) | copy-done | bytes 524312
  8.8 0.0 collective-permute-start
  8.8 8.1 %collective-permute-start.1 = (bf16[128,128]{1,0:T(8,128)(2,1)S(1)}, bf16[128,128]{1,0:T(8,128)(2,1)S(1)}, u32[]{:S(2)}, u32[]{:S(2)}) collective-permute-start(bf16[128,128]{1,0:T(8,128)(2,1)S(1)} %get-tuple-element.13), channel_id=1, source_target_pairs={{4,8},{8,4},{12,16},{16,12},{20,24},{24,20},{28,32},{32,28},{36,40... | collective-permute-start | bytes 98312 | tf_op jit(solution)/shard_map/ppermute | solution.py:243
  17.0 0.1 collective-permute-start.2
  17.1 3.9 %collective-permute-start.3 = (bf16[128,128]{1,0:T(8,128)(2,1)S(1)}, bf16[128,128]{1,0:T(8,128)(2,1)S(1)}, u32[]{:S(2)}, u32[]{:S(2)}) collective-permute-start(bf16[128,128]{1,0:T(8,128)(2,1)S(1)} %get-tuple-element.15), channel_id=1, source_target_pairs={{8,16},{16,8},{12,20},{20,12},{24,32},{32,24},{28,36},{36,28},{40,... | collective-permute-start | bytes 98312 | tf_op jit(solution)/shard_map/ppermute | solution.py:252
  21.0 1.1 %fusion.2.var = s32[1,128]{1,0:T(1,128)} fusion(s32[128]{0:T(128)} %param.16, s32[]{:T(128)S(6)} %select_n.43, s32[]{:T(128)S(6)} %axis_index.15), kind=kLoop, calls=%fused_computation.13 | loop fusion | flops 3328 | bytes 1032 | tf_op jit(solution)/shard_map/reshape | solution.py:274
  22.1 0.0 collective-permute-done.ghost0
  22.2 0.0 copy-start.6
  22.2 0.0 collective-permute-done.1.ghost1
  22.2 0.0 copy-start.7
  22.2 0.0 collective-permute-done.2.ghost2
  22.2 0.0 copy-start.8
  22.2 2.8 %collective-permute-done.3.ghost3 = bf16[128,128]{1,0:T(8,128)(2,1)S(1)} collective-permute-done((bf16[128,128]{1,0:T(8,128)(2,1)S(1)}, bf16[128,128]{1,0:T(8,128)(2,1)S(1)}, u32[]{:S(2)}, u32[]{:S(2)}) %collective-permute-start.3) | collective-permute-done | bytes 32800 | tf_op jit(solution)/shard_map/ppermute | solution.py:252
  25.0 0.0 copy-start.9
  25.0 1.3 %broadcast_in_dim.10.lam = f32[16,128]{1,0:T(8,128)} broadcast(f32[16]{0:T(128)} %param.13), dimensions={0} | broadcast | bytes 8256 | tf_op jit(solution)/shard_map/broadcast_in_dim | solution.py:271
  26.3 0.0 copy-done.4
  26.3 0.0 copy-done.6
  26.4 0.0 copy-done.7
  26.4 0.0 copy-done.8
  26.4 0.0 copy-done.9
  26.4 25.8 %shard_map.105 = (f32[16,128]{1,0:T(8,128)}, f32[16,128]{1,0:T(8,128)}, f32[16,128]{1,0:T(8,128)}) custom-call(f32[4096,128]{1,0:T(8,128)} %copy-done, bf16[128,128]{1,0:T(8,128)(2,1)} %copy-done.6, bf16[128,128]{1,0:T(8,128)(2,1)} %copy-done.7, bf16[128,128]{1,0:T(8,128)(2,1)} %copy-done.8, bf16[128,128]{1,0:T(8,128)(2,1)} %copy-done.9, s32[4]{0:T(128)} %copy-done.4, ...), custom_call_target="tpu_custom_call" | custom-call | tf_op jit(solution)/shard_map/pallas_call | solution.py:217
  52.2 0.1 collective-permute-start.4
  52.3 4.0 %collective-permute-start.5 = (f32[16,128]{1,0:T(8,128)}, f32[16,128]{1,0:T(8,128)S(1)}, u32[]{:S(2)}, u32[]{:S(2)}) collective-permute-start(f32[16,128]{1,0:T(8,128)} %get-tuple-element.19), channel_id=1, source_target_pairs={{4,8},{8,4},{12,16},{16,12},{20,24},{24,20},{28,32},{32,28},{36,40... | collective-permute-start | bytes 24584 | tf_op jit(solution)/shard_map/ppermute | solution.py:243
  56.2 0.0 collective-permute-done.4
  56.3 3.3 %collective-permute-done.5 = f32[16,128]{1,0:T(8,128)S(1)} collective-permute-done((f32[16,128]{1,0:T(8,128)}, f32[16,128]{1,0:T(8,128)S(1)}, u32[]{:S(2)}, u32[]{:S(2)}) %collective-permute-start.5) | collective-permute-done | bytes 8224 | tf_op jit(solution)/shard_map/ppermute | solution.py:243
  59.6 0.0 copy-done.10
  59.6 1.3 %multiply_reduce_fusion = (f32[128]{0:T(128)S(1)}, f32[16,128]{1,0:T(8,128)}) fusion(f32[16]{0:T(128)S(1)} %copy-done.10, f32[16,128]{1,0:T(8,128)S(1)} %collective-permute-done.5, f32[16,128]{1,0:T(8,128)} %get-tuple-element.17, f32[16,128]{1,0:T(8,128)S(1)} %collective-permute-done.4), kind=kLoop, calls=%fused_computation | loop fusion | flops 8064 | bytes 33344 | tf_op jit(solution)/shard_map/reduce_sum | solution.py:276
  60.9 1.6 %collective-permute-start.6 = (f32[128]{0:T(128)S(1)}, f32[128]{0:T(128)S(1)}, u32[]{:S(2)}, u32[]{:S(2)}) collective-permute-start(f32[128]{0:T(128)S(1)} %get-tuple-element.20), channel_id=1, source_target_pairs={{0,1},{1,0},{2,3},{3,2},{4,5},{5,4},{6,7},{7,6},{8,9},{9,8},{10,11... | collective-permute-start | bytes 1544 | tf_op jit(solution)/shard_map/ppermute | solution.py:277
  62.5 2.9 %collective-permute-start.7 = (f32[128]{0:T(128)S(1)}, f32[128]{0:T(128)S(1)}, u32[]{:S(2)}, u32[]{:S(2)}) collective-permute-start(f32[128]{0:T(128)S(1)} %get-tuple-element.20), channel_id=1, source_target_pairs={{0,2},{1,3},{2,0},{3,1},{4,6},{5,7},{6,4},{7,5},{8,10},{9,11},{10,... | collective-permute-start | bytes 1544 | tf_op jit(solution)/shard_map/ppermute | solution.py:277
  65.4 0.2 collective-permute-start.8
  65.6 0.0 collective-permute-done.6
  65.6 1.9 %collective-permute-done.7 = f32[128]{0:T(128)S(1)} collective-permute-done((f32[128]{0:T(128)S(1)}, f32[128]{0:T(128)S(1)}, u32[]{:S(2)}, u32[]{:S(2)}) %collective-permute-start.7) | collective-permute-done | bytes 544 | tf_op jit(solution)/shard_map/ppermute | solution.py:277
  67.5 2.6 %collective-permute-done.8 = f32[128]{0:T(128)S(1)} collective-permute-done((f32[128]{0:T(128)S(1)}, f32[128]{0:T(128)S(1)}, u32[]{:S(2)}, u32[]{:S(2)}) %collective-permute-start.8) | collective-permute-done | bytes 544 | tf_op jit(solution)/shard_map/ppermute | solution.py:277
  70.1 0.5 add_add_fusion.1
Async XLA Ops:
  0.6 58.9 %copy-start.10 = (f32[16]{0:T(128)S(1)}, f32[16]{0:T(128)}, u32[]{:S(2)}) copy-start(f32[16]{0:T(128)} %param.17) | copy-start | bytes 196
  0.8 25.6 %copy-start.4 = (s32[4]{0:T(128)}, s32[4]{0:T(128)S(1)}, u32[]{:S(2)}) copy-start(s32[4]{0:T(128)S(1)} %pad_add_fusion.order) | copy-start | bytes 52
  0.8 1.1 %copy-start.1 = (bf16[6,16,4096]{2,1,0:T(8,128)(2,1)S(1)}, bf16[6,16,4096]{2,1,0:T(8,128)(2,1)}, u32[]{:S(2)}) copy-start(bf16[6,16,4096]{2,1,0:T(8,128)(2,1)} %param.9) | copy-start | bytes 2359300
  1.9 0.7 %copy-start.3 = (bf16[6,4,6,4]{2,3,1,0:T(4,128)(2,1)S(1)}, bf16[6,4,6,4]{2,3,1,0:T(4,128)(2,1)}, u32[]{:S(2)}) copy-start(bf16[6,4,6,4]{2,3,1,0:T(4,128)(2,1)} %param.11) | copy-start | bytes 3460
  2.6 0.7 copy-start.5
  6.7 1.3 %copy-start = (f32[4096,128]{1,0:T(8,128)}, f32[4096,128]{1,0:T(8,128)S(1)}, u32[]{:S(2)}) copy-start(f32[4096,128]{1,0:T(8,128)S(1)} %get-tuple-element.11.table_in) | copy-start | bytes 6291460
  8.1 0.8 %copy-start.2 = (bf16[512,512]{1,0:T(8,128)(2,1)}, bf16[512,512]{1,0:T(8,128)(2,1)S(1)}, u32[]{:S(2)}) copy-start(bf16[512,512]{1,0:T(8,128)(2,1)S(1)} %get-tuple-element.16.weights) | copy-start | bytes 1572868
  8.8 13.3 %collective-permute-start = (bf16[128,128]{1,0:T(8,128)(2,1)S(1)}, bf16[128,128]{1,0:T(8,128)(2,1)S(1)}, u32[]{:S(2)}, u32[]{:S(2)}) collective-permute-start(bf16[128,128]{1,0:T(8,128)(2,1)S(1)} %get-tuple-element.12), channel_id=1, source_target_pairs={{0,4},{4,0},{8,12},{12,8},{16,20},{20,16},{24,28},{28,24},{32,36},... | collective-permute-start | bytes 98312 | tf_op jit(solution)/shard_map/ppermute | solution.py:243
  8.8 13.3 %collective-permute-start.1 = (bf16[128,128]{1,0:T(8,128)(2,1)S(1)}, bf16[128,128]{1,0:T(8,128)(2,1)S(1)}, u32[]{:S(2)}, u32[]{:S(2)}) collective-permute-start(bf16[128,128]{1,0:T(8,128)(2,1)S(1)} %get-tuple-element.13), channel_id=1, source_target_pairs={{4,8},{8,4},{12,16},{16,12},{20,24},{24,20},{28,32},{32,28},{36,40... | collective-permute-start | bytes 98312 | tf_op jit(solution)/shard_map/ppermute | solution.py:243
  17.0 5.2 %collective-permute-start.2 = (bf16[128,128]{1,0:T(8,128)(2,1)S(1)}, bf16[128,128]{1,0:T(8,128)(2,1)S(1)}, u32[]{:S(2)}, u32[]{:S(2)}) collective-permute-start(bf16[128,128]{1,0:T(8,128)(2,1)S(1)} %get-tuple-element.14), channel_id=1, source_target_pairs={{0,8},{8,0},{4,12},{12,4},{16,24},{24,16},{20,28},{28,20},{32,40},... | collective-permute-start | bytes 98312 | tf_op jit(solution)/shard_map/ppermute | solution.py:252
  17.1 7.9 %collective-permute-start.3 = (bf16[128,128]{1,0:T(8,128)(2,1)S(1)}, bf16[128,128]{1,0:T(8,128)(2,1)S(1)}, u32[]{:S(2)}, u32[]{:S(2)}) collective-permute-start(bf16[128,128]{1,0:T(8,128)(2,1)S(1)} %get-tuple-element.15), channel_id=1, source_target_pairs={{8,16},{16,8},{12,20},{20,12},{24,32},{32,24},{28,36},{36,28},{40,... | collective-permute-start | bytes 98312 | tf_op jit(solution)/shard_map/ppermute | solution.py:252
  22.2 4.2 %copy-start.6 = (bf16[128,128]{1,0:T(8,128)(2,1)}, bf16[128,128]{1,0:T(8,128)(2,1)S(1)}, u32[]{:S(2)}) copy-start(bf16[128,128]{1,0:T(8,128)(2,1)S(1)} %collective-permute-done.ghost0) | copy-start | bytes 98308
  22.2 4.2 %copy-start.7 = (bf16[128,128]{1,0:T(8,128)(2,1)}, bf16[128,128]{1,0:T(8,128)(2,1)S(1)}, u32[]{:S(2)}) copy-start(bf16[128,128]{1,0:T(8,128)(2,1)S(1)} %collective-permute-done.1.ghost1) | copy-start | bytes 98308
  22.2 4.2 %copy-start.8 = (bf16[128,128]{1,0:T(8,128)(2,1)}, bf16[128,128]{1,0:T(8,128)(2,1)S(1)}, u32[]{:S(2)}) copy-start(bf16[128,128]{1,0:T(8,128)(2,1)S(1)} %collective-permute-done.2.ghost2) | copy-start | bytes 98308
  25.0 1.4 %copy-start.9 = (bf16[128,128]{1,0:T(8,128)(2,1)}, bf16[128,128]{1,0:T(8,128)(2,1)S(1)}, u32[]{:S(2)}) copy-start(bf16[128,128]{1,0:T(8,128)(2,1)S(1)} %collective-permute-done.3.ghost3) | copy-start | bytes 98308
  52.2 4.1 %collective-permute-start.4 = (f32[16,128]{1,0:T(8,128)}, f32[16,128]{1,0:T(8,128)S(1)}, u32[]{:S(2)}, u32[]{:S(2)}) collective-permute-start(f32[16,128]{1,0:T(8,128)} %get-tuple-element.18), channel_id=1, source_target_pairs={{0,4},{4,0},{8,12},{12,8},{16,20},{20,16},{24,28},{28,24},{32,36},... | collective-permute-start | bytes 24584 | tf_op jit(solution)/shard_map/ppermute | solution.py:243
  52.3 7.3 %collective-permute-start.5 = (f32[16,128]{1,0:T(8,128)}, f32[16,128]{1,0:T(8,128)S(1)}, u32[]{:S(2)}, u32[]{:S(2)}) collective-permute-start(f32[16,128]{1,0:T(8,128)} %get-tuple-element.19), channel_id=1, source_target_pairs={{4,8},{8,4},{12,16},{16,12},{20,24},{24,20},{28,32},{32,28},{36,40... | collective-permute-start | bytes 24584 | tf_op jit(solution)/shard_map/ppermute | solution.py:243
  60.9 4.7 %collective-permute-start.6 = (f32[128]{0:T(128)S(1)}, f32[128]{0:T(128)S(1)}, u32[]{:S(2)}, u32[]{:S(2)}) collective-permute-start(f32[128]{0:T(128)S(1)} %get-tuple-element.20), channel_id=1, source_target_pairs={{0,1},{1,0},{2,3},{3,2},{4,5},{5,4},{6,7},{7,6},{8,9},{9,8},{10,11... | collective-permute-start | bytes 1544 | tf_op jit(solution)/shard_map/ppermute | solution.py:277
  62.5 5.0 %collective-permute-start.7 = (f32[128]{0:T(128)S(1)}, f32[128]{0:T(128)S(1)}, u32[]{:S(2)}, u32[]{:S(2)}) collective-permute-start(f32[128]{0:T(128)S(1)} %get-tuple-element.20), channel_id=1, source_target_pairs={{0,2},{1,3},{2,0},{3,1},{4,6},{5,7},{6,4},{7,5},{8,10},{9,11},{10,... | collective-permute-start | bytes 1544 | tf_op jit(solution)/shard_map/ppermute | solution.py:277
  65.4 4.8 %collective-permute-start.8 = (f32[128]{0:T(128)S(1)}, f32[128]{0:T(128)S(1)}, u32[]{:S(2)}, u32[]{:S(2)}) collective-permute-start(f32[128]{0:T(128)S(1)} %get-tuple-element.20), channel_id=1, source_target_pairs={{0,3},{1,2},{2,1},{3,0},{4,7},{5,6},{6,5},{7,4},{8,11},{9,10},{10,... | collective-permute-start | bytes 1544 | tf_op jit(solution)/shard_map/ppermute | solution.py:277

commit v3 on v2

--- a/solution.py
+++ b/solution.py
@@ -43,45 +43,33 @@
         weights[d * 128:d * 128 + 128, :] = jnp.where(same, block, 0.0).astype(bf16)
 
 
-def send_kernel(modes, send_list, order, mass, out0, out1, out2, out3, table, weights,
-                near, lists, stage, sem, list_sem):
-    nodes = modes.shape[1]
-    width = nodes // 4
-
-    def copy(n):
-        return pltpu.make_async_copy(modes.at[:, pl.ds(n * width, width)], near.at[:, pl.ds(n * width, width)], sem.at[n])
-
-    for n in range(4):
-        copy(n).start()
-    list_copy = pltpu.make_async_copy(send_list, lists, list_sem)
-    list_copy.start()
-    mass_matrix(mass, stage, weights)
-    for n in range(4):
-        copy(n).wait()
-
-        def transpose(q, _):
-            col = pl.ds(pl.multiple_of(n * width + q * TILE, TILE), TILE)
-            x = jnp.concatenate([near[:, col].astype(f32), jnp.zeros((32, TILE), f32)], axis=0)
-            table[col, :] = x.T
-            return 0
-
-        lax.fori_loop(0, width // TILE, transpose, 0, unroll=4)
-    list_copy.wait()
+def fill_table(modes, table):
+    def transpose(q, _):
+        col = pl.ds(pl.multiple_of(q * TILE, TILE), TILE)
+        x = jnp.concatenate([modes[:, col].astype(f32), jnp.zeros((32, TILE), f32)], axis=0)
+        table[col, :] = x.T
+        return 0
+
+    lax.fori_loop(0, modes.shape[1] // TILE, transpose, 0, unroll=8)
+
+
+def send_kernel(modes, send_list, order, out0, out1, out2, out3, table):
+    fill_table(modes, table)
     for d, out in enumerate((out0, out1, out2, out3)):
         which = order[d]
 
         def rows16(s, _):
-            rows = [table[pl.ds(lists[which, s * 16 + r], 1), :] for r in range(16)]
+            rows = [table[pl.ds(send_list[which, s * 16 + r], 1), :] for r in range(16)]
             out[pl.ds(pl.multiple_of(s * 16, 16), 16), :] = jnp.concatenate(rows, axis=0).astype(bf16)
             return 0
 
         lax.fori_loop(0, SLOTS // 16, rows16, 0, unroll=2)
 
 
-def main_kernel(table_in, ghost0, ghost1, ghost2, ghost3, order, stiff, weights, areas, lam, connect, var,
-                own, near, far, table, gather_a, gather_b, f_bufs, s_bufs, u_bufs, mass_rows, masses,
+def main_kernel(modes, ghost0, ghost1, ghost2, ghost3, order, stiff, mass_ref, areas, eigenvalues, connect, variables,
+                own, near, far, stage, weights, lam, table, gather_a, gather_b, f_bufs, s_bufs, u_bufs, mass_rows, masses,
                 index_a, index_b, stiff_near, energies, blocks, stiff_sem, index_sem):
-    nodes = table_in.shape[0]
+    nodes = modes.shape[1]
     chunks = connect.shape[1] // CHUNK
     gathers, indices = (gather_a, gather_b), (index_a, index_b)
 
@@ -98,7 +86,13 @@
     index_copy(1, 1).start()
     for n in range(chunks * TILES):
         stiff_copy(n).start()
-    table[0:nodes, :] = table_in[...]
+    mass_matrix(mass_ref, stage, weights)
+    row = iota((16, 128), 0)
+    scale = jnp.zeros((16, 128), f32)
+    for m in range(16):
+        scale = jnp.where(row == m, eigenvalues[m], scale)
+    lam[...] = scale
+    fill_table(modes, table)
     for d, ghost in enumerate((ghost0, ghost1, ghost2, ghost3)):
         place = pl.multiple_of(nodes + order[d ^ 1] * SLOTS, SLOTS)
         table[pl.ds(place, SLOTS), :] = ghost[...].astype(f32)
@@ -185,7 +179,10 @@
     add_blocks(chunks - 1)
     for slot in range(2):
         index_copy(0, slot).wait()
-    columns = (iota((3 * VAR_DEV, 128), 0) == var[...]).astype(bf16)
+    step = variables[...] // VAR_DEV - order[4]
+    place = jnp.where(step == 0, 0, jnp.where(step == 1 - 2 * order[0], 1, 2))
+    var = variables[...] % VAR_DEV + VAR_DEV * place
+    columns = (iota((3 * VAR_DEV, 128), 0) == var).astype(bf16)
     window = lax.dot_general(pieces(blocks[...]), columns, NT, preferred_element_type=f32)
     window = window[0:16] + window[16:32] + window[32:48]
     for part, out in enumerate((own, near, far)):
@@ -197,29 +194,25 @@
 HB = pl.BlockSpec(memory_space=pltpu.HBM)
 
 
-def send_rows(modes, send_list, order, mass_ref):
-    nodes = modes.shape[1]
+def send_rows(modes, send_list, order):
     return pl.pallas_call(
         send_kernel,
-        out_shape=[jax.ShapeDtypeStruct((SLOTS, 128), bf16)] * 4
-        + [jax.ShapeDtypeStruct((nodes, 128), f32), jax.ShapeDtypeStruct((512, 512), bf16)],
-        in_specs=[HB, HB, SM, VM], out_specs=[VM] * 6,
-        scratch_shapes=[
-            pltpu.VMEM(modes.shape, bf16), pltpu.SMEM(send_list.shape, jnp.int32), pltpu.VMEM((96, 128), f32),
-            pltpu.SemaphoreType.DMA((4,)), pltpu.SemaphoreType.DMA,
-        ],
+        out_shape=[jax.ShapeDtypeStruct((SLOTS, 128), bf16)] * 4,
+        in_specs=[VM, SM, SM], out_specs=[VM] * 4,
+        scratch_shapes=[pltpu.VMEM((modes.shape[1], 128), f32)],
         compiler_params=pltpu.CompilerParams(vmem_limit_bytes=12 * 2**20),
-    )(modes, send_list, order, mass_ref.transpose(0, 1, 3, 2))
-
-
-def main_call(table, ghosts, order, stiff, weights, areas, lam, connect, var):
+    )(modes, send_list, order)
+
+
+def main_call(modes, ghosts, order, stiff, mass_ref, areas, eigenvalues, connect, variables):
     chunks = connect.shape[1] // CHUNK
     return pl.pallas_call(
         main_kernel,
         out_shape=[jax.ShapeDtypeStruct((16, VAR_DEV), f32)] * 3,
-        in_specs=[VM, VM, VM, VM, VM, SM, HB, VM, VM, VM, HB, VM], out_specs=[VM] * 3,
+        in_specs=[VM, VM, VM, VM, VM, SM, HB, VM, VM, SM, HB, VM], out_specs=[VM] * 3,
         scratch_shapes=[
-            pltpu.VMEM((table.shape[0] + 4 * SLOTS, 128), f32),
+            pltpu.VMEM((96, 128), f32), pltpu.VMEM((512, 512), bf16), pltpu.VMEM((16, 128), f32),
+            pltpu.VMEM((modes.shape[1] + 4 * SLOTS, 128), f32),
             pltpu.VMEM((4, CHUNK, 128), f32), pltpu.VMEM((4, CHUNK, 128), f32),
             pltpu.VMEM((TILES, 576, 128), f32), pltpu.VMEM((TILES, 576, 128), f32),
             pltpu.VMEM((TILES, 4, 128, 128), f32), pltpu.VMEM((CHUNK, 512), f32), pltpu.VMEM((TILES, 16, 128), f32),
@@ -229,7 +222,7 @@
             pltpu.SemaphoreType.DMA((chunks * TILES,)), pltpu.SemaphoreType.DMA((2,)),
         ],
         compiler_params=pltpu.CompilerParams(vmem_limit_bytes=57 * 2**20),
-    )(table, *ghosts, order, stiff, weights, areas, lam, connect, var)
+    )(modes, *ghosts, order, stiff, mass_ref.transpose(0, 1, 3, 2), areas, eigenvalues, connect, variables)
 
 
 OFFSETS = (1, -1, 2, -2)
@@ -261,17 +254,13 @@
     flat = modes.reshape(6 * mode_dev, node_count)
     odd = region % 2
     upper = (region // 2) % 2
-    order = jnp.stack([odd, 1 - odd, 2 + upper, 3 - upper]).astype(jnp.int32)
-    *sent, table, weights = send_rows(flat, send_list, order, mass_ref)
+    order = jnp.stack([odd, 1 - odd, 2 + upper, 3 - upper, region]).astype(jnp.int32)
+    sent = send_rows(flat, send_list, order)
     received = [swap(sent[0], "region", 0), swap(sent[1], "region", 1),
                 swap_two(sent[2], "region", 0), swap_two(sent[3], "region", 1)]
-    step = block_var // VAR_DEV - region
-    near = jnp.where(odd == 1, -1, 1)
-    column = block_var % VAR_DEV + VAR_DEV * jnp.where(step == 0, 0, jnp.where(step == near, 1, 2))
-    lam = jnp.broadcast_to(eigenvalues[:, None], (mode_dev, 128))
     own, sent_a, sent_b = main_call(
-        table, received, order, stiffness, weights, areas.reshape(elem_count // 128, 128),
-        lam, connect, column.reshape(1, 128))
+        flat, received, order, stiffness, mass_ref, areas.reshape(elem_count // 128, 128),
+        eigenvalues, connect, block_var.reshape(1, elem_count // 32))
     sens = own + swap(sent_a, "region", 0) + swap(sent_b, "region", 1)
     weighted = jnp.sum(mode_weight[:, None] * sens, axis=0)
     other = [lax.ppermute(weighted, "mode", [(q, q ^ by) for q in range(4)]) for by in (1, 2, 3)]

time: 71 us -> 64.9 us (0.914)
  local copies, waits for them, and re-layouts: 6.04 us -> 2.5 us
  Pallas kernels: 29.2 us -> 27.9 us
  other arithmetic: 3.04 us -> 1.82 us
    unnamed x22 -> x16, local copies, waits for them, and re-layouts: 4.7 us -> 2.42 us
    broadcast_in_dim x1 -> x0, local copies, waits for them, and re-layouts: 1.34 us -> none  [shards(): lam = jnp.broadcast_to(eigenvalues[:, None], (mode_dev, 128))]
    reshape x1 -> x0, other arithmetic: 1.15 us -> none  [shards(): column.reshape(1, 128)]
    ppermute x2, waiting for transfers between devices: 2.82 us -> 3.95 us  [swap_two(): return lax.ppermute(array, axis, pairs)]
    pallas_call x1, Pallas kernels: 3.39 us -> 2.33 us  [send_rows(): pl.pallas_call(send_kernel, out_shape=[jax.ShapeDtypeStruct((SLOTS, 128),...]
  transfers between devices with their start and end apart: 9 -> 9, of which waited for: 4 -> 4; matrix products, arithmetic and copies ran while one was open for 2% -> 0% of each run, Pallas kernels for 0% -> 0%
where the time goes in v3:
time: 64.9 us; the launch traced here: 64.6 us
  Pallas kernels  27.9 us (43%)
  starting transfers between devices  20.4 us (31%)
  waiting for transfers between devices  11.2 us (17%)
  local copies, waits for them, and re-layouts  2.5 us (4%)
  other arithmetic  1.82 us (3%)
  between operations  0.81 us (1%)
    pallas_call x1, Pallas kernels, main_call(): pl.pallas_call(main_kernel, out_shape=[jax.ShapeDtypeStruct((16, VAR_DEV)...  25.5 us
    ppermute x4, starting transfers between devices, swap(): return lax.ppermute(array, axis, pairs)  12.3 us
    ppermute x3, starting transfers between devices, shards(): lax.ppermute(weighted, 'mode', [(q, q ^ by) for q in range(4)])  4.09 us
    ppermute x2, starting transfers between devices, swap_two(): return lax.ppermute(array, axis, pairs)  3.99 us
    ppermute x3, waiting for transfers between devices, shards(): lax.ppermute(weighted, 'mode', [(q, q ^ by) for q in range(4)])  3.96 us
    ppermute x2, waiting for transfers between devices, swap_two(): return lax.ppermute(array, axis, pairs)  3.95 us
    ppermute x4, waiting for transfers between devices, swap(): return lax.ppermute(array, axis, pairs)  3.29 us
    unnamed x16, local copies, waits for them, and re-layouts  2.42 us
  transfers between devices with their start and end apart: 9, of which 4 were waited for; matrix products, arithmetic and copies ran while one was open for 0% of the time, Pallas kernels for 0%

profile of v3, /device:TPU:6, one launch (start us, length us, event | category | flops | bytes accessed | tf_op | source)
XLA Modules:
  0.0 64.6 jit_solution(18272216436731762557)
XLA Ops:
  0.6 0.0 copy-start.7
  0.7 0.1 stack.23.order
  0.8 0.0 copy-start.1
  0.8 0.0 copy-start
  0.8 1.1 %copy-done = bf16[6,16,4096]{2,1,0:T(8,128)(2,1)S(1)} copy-done((bf16[6,16,4096]{2,1,0:T(8,128)(2,1)S(1)}, bf16[6,16,4096]{2,1,0:T(8,128)(2,1)}, u32[]{:S(2)}) %copy-start) | copy-done | bytes 786456
  1.9 0.0 copy-start.2
  1.9 0.7 %copy-done.2 = s32[4,128]{1,0:T(4,128)S(1)} copy-done((s32[4,128]{1,0:T(4,128)S(1)}, s32[4,128]{1,0:T(4,128)}, u32[]{:S(2)}) %copy-start.2) | copy-done | bytes 2072
  2.6 2.3 %shard_map.104 = (bf16[128,128]{1,0:T(8,128)(2,1)S(1)}, bf16[128,128]{1,0:T(8,128)(2,1)S(1)}, bf16[128,128]{1,0:T(8,128)(2,1)S(1)}, bf16[128,128]{1,0:T(8,128)(2,1)S(1)}) custom-call(bf16[96,4096]{1,0:T(8,128)(2,1)S(1)} %bitcast.10, s32[4,128]{1,0:T(4,128)S(1)} %copy-done.2, s32[5]{0:T(128)S(1)} %stack.23.order), custom_call_target="tpu_custom_call" | custom-call | tf_op jit(solution)/shard_map/pallas_call | solution.py:198
  4.9 0.1 collective-permute-start
  5.0 8.1 %collective-permute-start.1 = (bf16[128,128]{1,0:T(8,128)(2,1)S(1)}, bf16[128,128]{1,0:T(8,128)(2,1)S(1)}, u32[]{:S(2)}, u32[]{:S(2)}) collective-permute-start(bf16[128,128]{1,0:T(8,128)(2,1)S(1)} %get-tuple-element.10), channel_id=1, source_target_pairs={{4,8},{8,4},{12,16},{16,12},{20,24},{24,20},{28,32},{32,28},{36,40... | collective-permute-start | bytes 98312 | tf_op jit(solution)/shard_map/ppermute | solution.py:236
  13.1 0.1 collective-permute-start.2
  13.2 3.9 %collective-permute-start.3 = (bf16[128,128]{1,0:T(8,128)(2,1)S(1)}, bf16[128,128]{1,0:T(8,128)(2,1)S(1)}, u32[]{:S(2)}, u32[]{:S(2)}) collective-permute-start(bf16[128,128]{1,0:T(8,128)(2,1)S(1)} %get-tuple-element.12), channel_id=1, source_target_pairs={{8,16},{16,8},{12,20},{20,12},{24,32},{32,24},{28,36},{36,28},{40,... | collective-permute-start | bytes 98312 | tf_op jit(solution)/shard_map/ppermute | solution.py:245
  17.2 0.0 collective-permute-done.ghost0
  17.2 0.0 copy-start.3
  17.2 0.0 collective-permute-done.1.ghost1
  17.2 0.0 copy-start.4
  17.2 0.0 collective-permute-done.2.ghost2
  17.2 0.0 copy-start.5
  17.2 4.0 %collective-permute-done.3.ghost3 = bf16[128,128]{1,0:T(8,128)(2,1)S(1)} collective-permute-done((bf16[128,128]{1,0:T(8,128)(2,1)S(1)}, bf16[128,128]{1,0:T(8,128)(2,1)S(1)}, u32[]{:S(2)}, u32[]{:S(2)}) %collective-permute-start.3) | collective-permute-done | bytes 32800 | tf_op jit(solution)/shard_map/ppermute | solution.py:245
  21.2 0.0 copy-start.6
  21.2 0.0 copy-done.1
  21.2 0.0 copy-done.3
  21.2 0.0 copy-done.4
  21.2 0.0 copy-done.5
  21.2 0.6 copy-done.6
  21.8 25.5 %shard_map.105 = (f32[16,128]{1,0:T(8,128)}, f32[16,128]{1,0:T(8,128)}, f32[16,128]{1,0:T(8,128)}) custom-call(bf16[96,4096]{1,0:T(8,128)(2,1)} %bitcast.9, bf16[128,128]{1,0:T(8,128)(2,1)} %copy-done.3, bf16[128,128]{1,0:T(8,128)(2,1)} %copy-done.4, bf16[128,128]{1,0:T(8,128)(2,1)} %copy-done.5, bf16[128,128]{1,0:T(8,128)(2,1)} %copy-done.6, s32[5]{0:T(128)} %copy-done.1, ...), custom_call_target="tpu_custom_call" | custom-call | tf_op jit(solution)/shard_map/pallas_call | solution.py:209
  47.3 0.1 collective-permute-start.4
  47.4 4.0 %collective-permute-start.5 = (f32[16,128]{1,0:T(8,128)}, f32[16,128]{1,0:T(8,128)S(1)}, u32[]{:S(2)}, u32[]{:S(2)}) collective-permute-start(f32[16,128]{1,0:T(8,128)} %get-tuple-element.15), channel_id=1, source_target_pairs={{4,8},{8,4},{12,16},{16,12},{20,24},{24,20},{28,32},{32,28},{36,40... | collective-permute-start | bytes 24584 | tf_op jit(solution)/shard_map/ppermute | solution.py:236
  51.4 0.0 collective-permute-done.4
  51.4 3.3 %collective-permute-done.5 = f32[16,128]{1,0:T(8,128)S(1)} collective-permute-done((f32[16,128]{1,0:T(8,128)}, f32[16,128]{1,0:T(8,128)S(1)}, u32[]{:S(2)}, u32[]{:S(2)}) %collective-permute-start.5) | collective-permute-done | bytes 8224 | tf_op jit(solution)/shard_map/ppermute | solution.py:236
  54.7 0.0 copy-done.7
  54.7 1.3 %multiply_reduce_fusion = (f32[128]{0:T(128)S(1)}, f32[16,128]{1,0:T(8,128)}) fusion(f32[16]{0:T(128)S(1)} %copy-done.7, f32[16,128]{1,0:T(8,128)S(1)} %collective-permute-done.5, f32[16,128]{1,0:T(8,128)} %get-tuple-element.13, f32[16,128]{1,0:T(8,128)S(1)} %collective-permute-done.4), kind=kLoop, calls=%fused_computation | loop fusion | flops 8064 | bytes 33344 | tf_op jit(solution)/shard_map/reduce_sum | solution.py:265
  56.0 3.0 %collective-permute-start.8 = (f32[128]{0:T(128)S(1)}, f32[128]{0:T(128)S(1)}, u32[]{:S(2)}, u32[]{:S(2)}) collective-permute-start(f32[128]{0:T(128)S(1)} %get-tuple-element.16), channel_id=1, source_target_pairs={{0,3},{1,2},{2,1},{3,0},{4,7},{5,6},{6,5},{7,4},{8,11},{9,10},{10,... | collective-permute-start | bytes 1544 | tf_op jit(solution)/shard_map/ppermute | solution.py:266
  59.0 0.6 collective-permute-start.7
  59.6 0.5 collective-permute-start.6
  60.1 0.7 %collective-permute-done.8 = f32[128]{0:T(128)S(1)} collective-permute-done((f32[128]{0:T(128)S(1)}, f32[128]{0:T(128)S(1)}, u32[]{:S(2)}, u32[]{:S(2)}) %collective-permute-start.8) | collective-permute-done | bytes 544 | tf_op jit(solution)/shard_map/ppermute | solution.py:266
  60.8 3.3 %collective-permute-done.7 = f32[128]{0:T(128)S(1)} collective-permute-done((f32[128]{0:T(128)S(1)}, f32[128]{0:T(128)S(1)}, u32[]{:S(2)}, u32[]{:S(2)}) %collective-permute-start.7) | collective-permute-done | bytes 544 | tf_op jit(solution)/shard_map/ppermute | solution.py:266
  64.1 0.0 collective-permute-done.6
  64.1 0.5 add_add_fusion.1
Async XLA Ops:
  0.6 54.1 %copy-start.7 = (f32[16]{0:T(128)S(1)}, f32[16]{0:T(128)}, u32[]{:S(2)}) copy-start(f32[16]{0:T(128)} %param.17) | copy-start | bytes 196
  0.8 20.4 %copy-start.1 = (s32[5]{0:T(128)}, s32[5]{0:T(128)S(1)}, u32[]{:S(2)}) copy-start(s32[5]{0:T(128)S(1)} %stack.23.order) | copy-start | bytes 64
  0.8 1.1 %copy-start = (bf16[6,16,4096]{2,1,0:T(8,128)(2,1)S(1)}, bf16[6,16,4096]{2,1,0:T(8,128)(2,1)}, u32[]{:S(2)}) copy-start(bf16[6,16,4096]{2,1,0:T(8,128)(2,1)} %param.9) | copy-start | bytes 2359300
  1.9 0.7 %copy-start.2 = (s32[4,128]{1,0:T(4,128)S(1)}, s32[4,128]{1,0:T(4,128)}, u32[]{:S(2)}) copy-start(s32[4,128]{1,0:T(4,128)} %send_list.1) | copy-start | bytes 6148
  4.9 12.2 %collective-permute-start = (bf16[128,128]{1,0:T(8,128)(2,1)S(1)}, bf16[128,128]{1,0:T(8,128)(2,1)S(1)}, u32[]{:S(2)}, u32[]{:S(2)}) collective-permute-start(bf16[128,128]{1,0:T(8,128)(2,1)S(1)} %get-tuple-element.9), channel_id=1, source_target_pairs={{0,4},{4,0},{8,12},{12,8},{16,20},{20,16},{24,28},{28,24},{32,36},... | collective-permute-start | bytes 98312 | tf_op jit(solution)/shard_map/ppermute | solution.py:236
  5.0 12.2 %collective-permute-start.1 = (bf16[128,128]{1,0:T(8,128)(2,1)S(1)}, bf16[128,128]{1,0:T(8,128)(2,1)S(1)}, u32[]{:S(2)}, u32[]{:S(2)}) collective-permute-start(bf16[128,128]{1,0:T(8,128)(2,1)S(1)} %get-tuple-element.10), channel_id=1, source_target_pairs={{4,8},{8,4},{12,16},{16,12},{20,24},{24,20},{28,32},{32,28},{36,40... | collective-permute-start | bytes 98312 | tf_op jit(solution)/shard_map/ppermute | solution.py:236
  13.1 4.1 %collective-permute-start.2 = (bf16[128,128]{1,0:T(8,128)(2,1)S(1)}, bf16[128,128]{1,0:T(8,128)(2,1)S(1)}, u32[]{:S(2)}, u32[]{:S(2)}) collective-permute-start(bf16[128,128]{1,0:T(8,128)(2,1)S(1)} %get-tuple-element.11), channel_id=1, source_target_pairs={{0,8},{8,0},{4,12},{12,4},{16,24},{24,16},{20,28},{28,20},{32,40},... | collective-permute-start | bytes 98312 | tf_op jit(solution)/shard_map/ppermute | solution.py:245
  13.2 7.9 %collective-permute-start.3 = (bf16[128,128]{1,0:T(8,128)(2,1)S(1)}, bf16[128,128]{1,0:T(8,128)(2,1)S(1)}, u32[]{:S(2)}, u32[]{:S(2)}) collective-permute-start(bf16[128,128]{1,0:T(8,128)(2,1)S(1)} %get-tuple-element.12), channel_id=1, source_target_pairs={{8,16},{16,8},{12,20},{20,12},{24,32},{32,24},{28,36},{36,28},{40,... | collective-permute-start | bytes 98312 | tf_op jit(solution)/shard_map/ppermute | solution.py:245
  17.2 4.0 %copy-start.3 = (bf16[128,128]{1,0:T(8,128)(2,1)}, bf16[128,128]{1,0:T(8,128)(2,1)S(1)}, u32[]{:S(2)}) copy-start(bf16[128,128]{1,0:T(8,128)(2,1)S(1)} %collective-permute-done.ghost0) | copy-start | bytes 98308
  17.2 4.0 %copy-start.4 = (bf16[128,128]{1,0:T(8,128)(2,1)}, bf16[128,128]{1,0:T(8,128)(2,1)S(1)}, u32[]{:S(2)}) copy-start(bf16[128,128]{1,0:T(8,128)(2,1)S(1)} %collective-permute-done.1.ghost1) | copy-start | bytes 98308
  17.2 4.0 %copy-start.5 = (bf16[128,128]{1,0:T(8,128)(2,1)}, bf16[128,128]{1,0:T(8,128)(2,1)S(1)}, u32[]{:S(2)}) copy-start(bf16[128,128]{1,0:T(8,128)(2,1)S(1)} %collective-permute-done.2.ghost2) | copy-start | bytes 98308
  21.2 0.6 copy-start.6
  47.3 4.1 %collective-permute-start.4 = (f32[16,128]{1,0:T(8,128)}, f32[16,128]{1,0:T(8,128)S(1)}, u32[]{:S(2)}, u32[]{:S(2)}) collective-permute-start(f32[16,128]{1,0:T(8,128)} %get-tuple-element.14), channel_id=1, source_target_pairs={{0,4},{4,0},{8,12},{12,8},{16,20},{20,16},{24,28},{28,24},{32,36},... | collective-permute-start | bytes 24584 | tf_op jit(solution)/shard_map/ppermute | solution.py:236
  47.4 7.3 %collective-permute-start.5 = (f32[16,128]{1,0:T(8,128)}, f32[16,128]{1,0:T(8,128)S(1)}, u32[]{:S(2)}, u32[]{:S(2)}) collective-permute-start(f32[16,128]{1,0:T(8,128)} %get-tuple-element.15), channel_id=1, source_target_pairs={{4,8},{8,4},{12,16},{16,12},{20,24},{24,20},{28,32},{32,28},{36,40... | collective-permute-start | bytes 24584 | tf_op jit(solution)/shard_map/ppermute | solution.py:236
  56.0 4.8 %collective-permute-start.8 = (f32[128]{0:T(128)S(1)}, f32[128]{0:T(128)S(1)}, u32[]{:S(2)}, u32[]{:S(2)}) collective-permute-start(f32[128]{0:T(128)S(1)} %get-tuple-element.16), channel_id=1, source_target_pairs={{0,3},{1,2},{2,1},{3,0},{4,7},{5,6},{6,5},{7,4},{8,11},{9,10},{10,... | collective-permute-start | bytes 1544 | tf_op jit(solution)/shard_map/ppermute | solution.py:266
  59.0 5.0 %collective-permute-start.7 = (f32[128]{0:T(128)S(1)}, f32[128]{0:T(128)S(1)}, u32[]{:S(2)}, u32[]{:S(2)}) collective-permute-start(f32[128]{0:T(128)S(1)} %get-tuple-element.16), channel_id=1, source_target_pairs={{0,2},{1,3},{2,0},{3,1},{4,6},{5,7},{6,4},{7,5},{8,10},{9,11},{10,... | collective-permute-start | bytes 1544 | tf_op jit(solution)/shard_map/ppermute | solution.py:266
  59.6 4.4 %collective-permute-start.6 = (f32[128]{0:T(128)S(1)}, f32[128]{0:T(128)S(1)}, u32[]{:S(2)}, u32[]{:S(2)}) collective-permute-start(f32[128]{0:T(128)S(1)} %get-tuple-element.16), channel_id=1, source_target_pairs={{0,1},{1,0},{2,3},{3,2},{4,5},{5,4},{6,7},{7,6},{8,9},{9,8},{10,11... | collective-permute-start | bytes 1544 | tf_op jit(solution)/shard_map/ppermute | solution.py:266

commit v4 on v3

--- a/solution.py
+++ b/solution.py
@@ -30,7 +30,7 @@
     for a in range(6):
         for c in range(4):
             first = (a * 4 + c) * 4
-            stage[first:first + 4, 0:6] = mass[a, c].astype(f32)
+            stage[first:first + 4, 0:6] = mass[a, c]
     values = stage[...].astype(bf16)
     col = iota((512, 96), 0)
     comp, corner = (col % 128) // 16, col // 128
@@ -66,10 +66,10 @@
         lax.fori_loop(0, SLOTS // 16, rows16, 0, unroll=2)
 
 
-def main_kernel(modes, ghost0, ghost1, ghost2, ghost3, order, stiff, mass_ref, areas, eigenvalues, connect, variables,
-                own, near, far, stage, weights, lam, table, gather_a, gather_b, f_bufs, s_bufs, u_bufs, mass_rows, masses,
+def main_kernel(rows_in, ghost0, ghost1, ghost2, ghost3, order, stiff, mass_ref, minus_areas, lam, connect, var,
+                own, near, far, stage, weights, table, gather_a, gather_b, f_bufs, s_bufs, u_bufs, mass_rows, masses,
                 index_a, index_b, stiff_near, energies, blocks, stiff_sem, index_sem):
-    nodes = modes.shape[1]
+    nodes = rows_in.shape[0]
     chunks = connect.shape[1] // CHUNK
     gathers, indices = (gather_a, gather_b), (index_a, index_b)
 
@@ -87,12 +87,7 @@
     for n in range(chunks * TILES):
         stiff_copy(n).start()
     mass_matrix(mass_ref, stage, weights)
-    row = iota((16, 128), 0)
-    scale = jnp.zeros((16, 128), f32)
-    for m in range(16):
-        scale = jnp.where(row == m, eigenvalues[m], scale)
-    lam[...] = scale
-    fill_table(modes, table)
+    table[0:nodes, :] = rows_in[...]
     for d, ghost in enumerate((ghost0, ghost1, ghost2, ghost3)):
         place = pl.multiple_of(nodes + order[d ^ 1] * SLOTS, SLOTS)
         table[pl.ds(place, SLOTS), :] = ghost[...].astype(f32)
@@ -139,8 +134,8 @@
                     acc = acc + s_buf[i * 24 + j:i * 24 + j + 1, :] * u[j]
                 total = acc * u[i] if total is None else total + acc * u[i]
             halves.append(total)
-        area = areas[pl.ds(n * TILES + q, 1), :]
-        energies[n, q] = jnp.concatenate(halves, axis=0) - lam[...] * area * masses[q]
+        area = minus_areas[pl.ds(n * TILES + q, 1), :]
+        energies[n, q] = jnp.concatenate(halves, axis=0) + lam[...] * area * masses[q]
 
     def add_blocks(n):
         values = jnp.concatenate([pieces(energies[n, q]) for q in range(TILES)], axis=0)
@@ -179,10 +174,7 @@
     add_blocks(chunks - 1)
     for slot in range(2):
         index_copy(0, slot).wait()
-    step = variables[...] // VAR_DEV - order[4]
-    place = jnp.where(step == 0, 0, jnp.where(step == 1 - 2 * order[0], 1, 2))
-    var = variables[...] % VAR_DEV + VAR_DEV * place
-    columns = (iota((3 * VAR_DEV, 128), 0) == var).astype(bf16)
+    columns = (iota((3 * VAR_DEV, 128), 0) == var[...]).astype(bf16)
     window = lax.dot_general(pieces(blocks[...]), columns, NT, preferred_element_type=f32)
     window = window[0:16] + window[16:32] + window[32:48]
     for part, out in enumerate((own, near, far)):
@@ -197,22 +189,21 @@
 def send_rows(modes, send_list, order):
     return pl.pallas_call(
         send_kernel,
-        out_shape=[jax.ShapeDtypeStruct((SLOTS, 128), bf16)] * 4,
-        in_specs=[VM, SM, SM], out_specs=[VM] * 4,
-        scratch_shapes=[pltpu.VMEM((modes.shape[1], 128), f32)],
+        out_shape=[jax.ShapeDtypeStruct((SLOTS, 128), bf16)] * 4 + [jax.ShapeDtypeStruct((modes.shape[1], 128), f32)],
+        in_specs=[VM, SM, SM], out_specs=[VM] * 5,
         compiler_params=pltpu.CompilerParams(vmem_limit_bytes=12 * 2**20),
     )(modes, send_list, order)
 
 
-def main_call(modes, ghosts, order, stiff, mass_ref, areas, eigenvalues, connect, variables):
+def main_call(rows, ghosts, order, stiff, mass_ref, minus_areas, lam, connect, var):
     chunks = connect.shape[1] // CHUNK
     return pl.pallas_call(
         main_kernel,
         out_shape=[jax.ShapeDtypeStruct((16, VAR_DEV), f32)] * 3,
-        in_specs=[VM, VM, VM, VM, VM, SM, HB, VM, VM, SM, HB, VM], out_specs=[VM] * 3,
+        in_specs=[VM, VM, VM, VM, VM, SM, HB, VM, VM, VM, HB, VM], out_specs=[VM] * 3,
         scratch_shapes=[
-            pltpu.VMEM((96, 128), f32), pltpu.VMEM((512, 512), bf16), pltpu.VMEM((16, 128), f32),
-            pltpu.VMEM((modes.shape[1] + 4 * SLOTS, 128), f32),
+            pltpu.VMEM((96, 128), f32), pltpu.VMEM((512, 512), bf16),
+            pltpu.VMEM((rows.shape[0] + 4 * SLOTS, 128), f32),
             pltpu.VMEM((4, CHUNK, 128), f32), pltpu.VMEM((4, CHUNK, 128), f32),
             pltpu.VMEM((TILES, 576, 128), f32), pltpu.VMEM((TILES, 576, 128), f32),
             pltpu.VMEM((TILES, 4, 128, 128), f32), pltpu.VMEM((CHUNK, 512), f32), pltpu.VMEM((TILES, 16, 128), f32),
@@ -221,8 +212,8 @@
             pltpu.VMEM((chunks, TILES, 16, 128), f32), pltpu.VMEM((16, 128), f32),
             pltpu.SemaphoreType.DMA((chunks * TILES,)), pltpu.SemaphoreType.DMA((2,)),
         ],
-        compiler_params=pltpu.CompilerParams(vmem_limit_bytes=57 * 2**20),
-    )(modes, *ghosts, order, stiff, mass_ref.transpose(0, 1, 3, 2), areas, eigenvalues, connect, variables)
+        compiler_params=pltpu.CompilerParams(vmem_limit_bytes=50 * 2**20),
+    )(rows, *ghosts, order, stiff, mass_ref, minus_areas, lam, connect, var)
 
 
 OFFSETS = (1, -1, 2, -2)
@@ -254,13 +245,17 @@
     flat = modes.reshape(6 * mode_dev, node_count)
     odd = region % 2
     upper = (region // 2) % 2
-    order = jnp.stack([odd, 1 - odd, 2 + upper, 3 - upper, region]).astype(jnp.int32)
-    sent = send_rows(flat, send_list, order)
+    order = jnp.stack([odd, 1 - odd, 2 + upper, 3 - upper]).astype(jnp.int32)
+    *sent, rows = send_rows(flat, send_list, order)
     received = [swap(sent[0], "region", 0), swap(sent[1], "region", 1),
                 swap_two(sent[2], "region", 0), swap_two(sent[3], "region", 1)]
+    step = block_var // VAR_DEV - region
+    place = jnp.where(step == 0, 0, jnp.where(step == 1 - 2 * odd, 1, 2))
+    column = block_var % VAR_DEV + VAR_DEV * place
     own, sent_a, sent_b = main_call(
-        flat, received, order, stiffness, mass_ref, areas.reshape(elem_count // 128, 128),
-        eigenvalues, connect, block_var.reshape(1, elem_count // 32))
+        rows, received, order, stiffness, mass_ref.transpose(0, 1, 3, 2).astype(f32),
+        -areas.reshape(elem_count // 128, 128), jnp.broadcast_to(eigenvalues[:, None], (mode_dev, 128)),
+        jnp.minimum(connect, node_count + 4 * SLOTS - 1), column.reshape(1, elem_count // 32))
     sens = own + swap(sent_a, "region", 0) + swap(sent_b, "region", 1)
     weighted = jnp.sum(mode_weight[:, None] * sens, axis=0)
     other = [lax.ppermute(weighted, "mode", [(q, q ^ by) for q in range(4)]) for by in (1, 2, 3)]

time: 64.9 us -> 63.4 us (0.977)
  waiting for transfers between devices: 11.2 us -> 8.59 us
  other arithmetic: 1.82 us -> 4.19 us
  Pallas kernels: 27.9 us -> 25.9 us
    ppermute x2, waiting for transfers between devices: 3.95 us -> 0.98 us  [swap_two(): return lax.ppermute(array, axis, pairs)]
    pallas_call x1, Pallas kernels: 25.5 us -> 23.6 us  [main_call(): pl.pallas_call(main_kernel, out_shape=[jax.ShapeDtypeStruct((16, VAR_DEV)...]
    min x0 -> x1, other arithmetic: none -> 0.86 us  [shards(): jnp.minimum(connect, node_count + 4 * SLOTS - 1)]
    convert_element_type x0 -> x1, other arithmetic: none -> 0.74 us  [shards(): mass_ref.transpose(0, 1, 3, 2).astype(f32)]
    broadcast_in_dim x0 -> x1, local copies, waits for them, and re-layouts: none -> 0.72 us  [shards(): jnp.broadcast_to(eigenvalues[:, None], (mode_dev, 128))]
    neg x0 -> x1, other arithmetic: none -> 0.72 us  [shards(): -areas.reshape(elem_count // 128, 128)]
    reduce_sum x1, other arithmetic: 1.3 us -> 0.61 us  [shards(): weighted = jnp.sum(mode_weight[:, None] * sens, axis=0)]
    reshape x0 -> x1, other arithmetic: none -> 0.67 us  [shards(): column.reshape(1, elem_count // 32)]
  transfers between devices with their start and end apart: 9 -> 9, of which waited for: 4 -> 4; matrix products, arithmetic and copies ran while one was open for 0% -> 5% of each run, Pallas kernels for 0% -> 0%
where the time goes in v4:
time: 63.4 us; the launch traced here: 63 us
  Pallas kernels  25.9 us (41%)
  starting transfers between devices  21 us (33%)
  waiting for transfers between devices  8.59 us (14%)
  other arithmetic  4.19 us (7%)
  local copies, waits for them, and re-layouts  2.54 us (4%)
  between operations  0.79 us (1%)
    pallas_call x1, Pallas kernels, main_call(): pl.pallas_call(main_kernel, out_shape=[jax.ShapeDtypeStruct((16, VAR_DEV)...  23.6 us
    ppermute x4, starting transfers between devices, swap(): return lax.ppermute(array, axis, pairs)  12.3 us
    ppermute x3, starting transfers between devices, shards(): lax.ppermute(weighted, 'mode', [(q, q ^ by) for q in range(4)])  4.7 us
    ppermute x3, waiting for transfers between devices, shards(): lax.ppermute(weighted, 'mode', [(q, q ^ by) for q in range(4)])  4.53 us
    ppermute x2, starting transfers between devices, swap_two(): return lax.ppermute(array, axis, pairs)  3.99 us
    ppermute x4, waiting for transfers between devices, swap(): return lax.ppermute(array, axis, pairs)  3.08 us
    pallas_call x1, Pallas kernels, send_rows(): pl.pallas_call(send_kernel, out_shape=[jax.ShapeDtypeStruct((SLOTS, 128),...  2.37 us
    unnamed x6, local copies, waits for them, and re-layouts  1.82 us
  transfers between devices with their start and end apart: 9, of which 4 were waited for; matrix products, arithmetic and copies ran while one was open for 5% of the time, Pallas kernels for 0%

profile of v4, /device:TPU:6, one launch (start us, length us, event | category | flops | bytes accessed | tf_op | source)
XLA Modules:
  0.0 63.0 jit_solution(18028605138677150314)
XLA Ops:
  0.6 0.0 copy-start.2
  0.7 0.1 pad_add_fusion.order
  0.8 0.0 copy-start
  0.8 1.1 %copy-done = bf16[6,16,4096]{2,1,0:T(8,128)(2,1)S(1)} copy-done((bf16[6,16,4096]{2,1,0:T(8,128)(2,1)S(1)}, bf16[6,16,4096]{2,1,0:T(8,128)(2,1)}, u32[]{:S(2)}) %copy-start) | copy-done | bytes 786456
  1.9 0.0 copy-start.1
  1.9 0.7 %copy-done.1 = s32[4,128]{1,0:T(4,128)S(1)} copy-done((s32[4,128]{1,0:T(4,128)S(1)}, s32[4,128]{1,0:T(4,128)}, u32[]{:S(2)}) %copy-start.1) | copy-done | bytes 2072
  2.6 2.4 %shard_map.104 = (bf16[128,128]{1,0:T(8,128)(2,1)S(1)}, bf16[128,128]{1,0:T(8,128)(2,1)S(1)}, bf16[128,128]{1,0:T(8,128)(2,1)S(1)}, bf16[128,128]{1,0:T(8,128)(2,1)S(1)}, f32[4096,128]{1,0:T(8,128)S(1)}) custom-call(bf16[96,4096]{1,0:T(8,128)(2,1)S(1)} %bitcast.11, s32[4,128]{1,0:T(4,128)S(1)} %copy-done.1, s32[4]{0:T(128)S(1)} %pad_add_fusion.order), custom_call_target="tpu_custom_call" | custom-call | tf_op jit(solution)/shard_map/pallas_call | solution.py:190
  5.0 0.1 collective-permute-start
  5.1 8.1 %collective-permute-start.1 = (bf16[128,128]{1,0:T(8,128)(2,1)S(1)}, bf16[128,128]{1,0:T(8,128)(2,1)S(1)}, u32[]{:S(2)}, u32[]{:S(2)}) collective-permute-start(bf16[128,128]{1,0:T(8,128)(2,1)S(1)} %get-tuple-element.12), channel_id=1, source_target_pairs={{4,8},{8,4},{12,16},{16,12},{20,24},{24,20},{28,32},{32,28},{36,40... | collective-permute-start | bytes 98312 | tf_op jit(solution)/shard_map/ppermute | solution.py:227
  13.2 0.1 collective-permute-start.2
  13.3 3.9 %collective-permute-start.3 = (bf16[128,128]{1,0:T(8,128)(2,1)S(1)}, bf16[128,128]{1,0:T(8,128)(2,1)S(1)}, u32[]{:S(2)}, u32[]{:S(2)}) collective-permute-start(bf16[128,128]{1,0:T(8,128)(2,1)S(1)} %get-tuple-element.14), channel_id=1, source_target_pairs={{8,16},{16,8},{12,20},{20,12},{24,32},{32,24},{28,36},{36,28},{40,... | collective-permute-start | bytes 98312 | tf_op jit(solution)/shard_map/ppermute | solution.py:236
  17.2 0.9 %broadcast_minimum_fusion.connect = s32[4,4096]{1,0:T(4,128)S(1)} fusion(s32[4,4096]{1,0:T(4,128)} %param.15), kind=kLoop, calls=%fused_computation.1 | loop fusion | flops 16384 | bytes 131072 | tf_op jit(solution)/shard_map/min | solution.py:258
  18.1 0.7 %convert_bitcast_fusion.mass_ref = f32[6,4,4,6]{3,2,1,0:T(4,128)S(1)} fusion(bf16[6,4,6,4]{2,3,1,0:T(4,128)(2,1)} %param.11), kind=kLoop, calls=%fused_computation | loop fusion | flops 576 | bytes 3456 | tf_op jit(solution)/shard_map/convert_element_type | solution.py:256
  18.8 0.7 %negate_bitcast_fusion.minus_areas = f32[32,128]{1,0:T(8,128)S(1)} fusion(f32[4096]{0:T(1024)} %param.12), kind=kLoop, calls=%fused_computation.2 | loop fusion | flops 4096 | bytes 32768 | tf_op jit(solution)/shard_map/neg | solution.py:257
  19.5 0.7 %fusion.2.var = s32[1,128]{1,0:T(1,128)S(1)} fusion(s32[128]{0:T(128)} %param.16, s32[]{:T(128)S(6)} %sub.31, s32[]{:T(128)S(6)} %axis_index.15), kind=kLoop, calls=%fused_computation.16 | loop fusion | flops 3328 | bytes 1032 | tf_op jit(solution)/shard_map/reshape | solution.py:258
  20.2 0.0 collective-permute-done.ghost0
  20.2 0.0 collective-permute-done.1.ghost1
  20.2 0.0 collective-permute-done.2.ghost2
  20.2 1.0 %collective-permute-done.3.ghost3 = bf16[128,128]{1,0:T(8,128)(2,1)S(1)} collective-permute-done((bf16[128,128]{1,0:T(8,128)(2,1)S(1)}, bf16[128,128]{1,0:T(8,128)(2,1)S(1)}, u32[]{:S(2)}, u32[]{:S(2)}) %collective-permute-start.3) | collective-permute-done | bytes 32800 | tf_op jit(solution)/shard_map/ppermute | solution.py:236
  21.2 0.7 %broadcast_in_dim.10.lam = f32[16,128]{1,0:T(8,128)S(1)} broadcast(f32[16]{0:T(128)} %param.13), dimensions={0} | broadcast | bytes 8256 | tf_op jit(solution)/shard_map/broadcast_in_dim | solution.py:257
  21.9 23.6 %shard_map.105 = (f32[16,128]{1,0:T(8,128)S(1)}, f32[16,128]{1,0:T(8,128)S(1)}, f32[16,128]{1,0:T(8,128)S(1)}) custom-call(f32[4096,128]{1,0:T(8,128)S(1)} %get-tuple-element.10.rows_in, bf16[128,128]{1,0:T(8,128)(2,1)S(1)} %collective-permute-done.ghost0, bf16[128,128]{1,0:T(8,128)(2,1)S(1)} %collective-permute-done.1.ghost1, ...), custom_call_target="tpu_custom_call" | custom-call | tf_op jit(solution)/shard_map/pallas_call | solution.py:200
  45.5 0.1 collective-permute-start.4
  45.6 4.0 %collective-permute-start.5 = (f32[16,128]{1,0:T(8,128)S(1)}, f32[16,128]{1,0:T(8,128)S(1)}, u32[]{:S(2)}, u32[]{:S(2)}) collective-permute-start(f32[16,128]{1,0:T(8,128)S(1)} %get-tuple-element.17), channel_id=1, source_target_pairs={{4,8},{8,4},{12,16},{16,12},{20,24},{24,20},{28,32},{32,28},{36,40... | collective-permute-start | bytes 24584 | tf_op jit(solution)/shard_map/ppermute | solution.py:227
  49.6 0.0 collective-permute-done.4
  49.6 3.1 %collective-permute-done.5 = f32[16,128]{1,0:T(8,128)S(1)} collective-permute-done((f32[16,128]{1,0:T(8,128)S(1)}, f32[16,128]{1,0:T(8,128)S(1)}, u32[]{:S(2)}, u32[]{:S(2)}) %collective-permute-start.5) | collective-permute-done | bytes 8224 | tf_op jit(solution)/shard_map/ppermute | solution.py:227
  52.7 0.0 copy-done.2
  52.7 0.6 multiply_reduce_fusion
  53.3 1.6 %collective-permute-start.6 = (f32[128]{0:T(128)S(1)}, f32[128]{0:T(128)S(1)}, u32[]{:S(2)}, u32[]{:S(2)}) collective-permute-start(f32[128]{0:T(128)S(1)} %get-tuple-element.18), channel_id=1, source_target_pairs={{0,1},{1,0},{2,3},{3,2},{4,5},{5,4},{6,7},{7,6},{8,9},{9,8},{10,11... | collective-permute-start | bytes 1544 | tf_op jit(solution)/shard_map/ppermute | solution.py:261
  54.9 2.9 %collective-permute-start.7 = (f32[128]{0:T(128)S(1)}, f32[128]{0:T(128)S(1)}, u32[]{:S(2)}, u32[]{:S(2)}) collective-permute-start(f32[128]{0:T(128)S(1)} %get-tuple-element.18), channel_id=1, source_target_pairs={{0,2},{1,3},{2,0},{3,1},{4,6},{5,7},{6,4},{7,5},{8,10},{9,11},{10,... | collective-permute-start | bytes 1544 | tf_op jit(solution)/shard_map/ppermute | solution.py:261
  57.8 0.2 collective-permute-start.8
  58.0 0.0 collective-permute-done.6
  58.0 1.9 %collective-permute-done.7 = f32[128]{0:T(128)S(1)} collective-permute-done((f32[128]{0:T(128)S(1)}, f32[128]{0:T(128)S(1)}, u32[]{:S(2)}, u32[]{:S(2)}) %collective-permute-start.7) | collective-permute-done | bytes 544 | tf_op jit(solution)/shard_map/ppermute | solution.py:261
  59.9 2.6 %collective-permute-done.8 = f32[128]{0:T(128)S(1)} collective-permute-done((f32[128]{0:T(128)S(1)}, f32[128]{0:T(128)S(1)}, u32[]{:S(2)}, u32[]{:S(2)}) %collective-permute-start.8) | collective-permute-done | bytes 544 | tf_op jit(solution)/shard_map/ppermute | solution.py:261
  62.5 0.5 add_add_fusion.1
Async XLA Ops:
  0.6 52.1 %copy-start.2 = (f32[16]{0:T(128)S(1)}, f32[16]{0:T(128)}, u32[]{:S(2)}) copy-start(f32[16]{0:T(128)} %param.17) | copy-start | bytes 196
  0.8 1.1 %copy-start = (bf16[6,16,4096]{2,1,0:T(8,128)(2,1)S(1)}, bf16[6,16,4096]{2,1,0:T(8,128)(2,1)}, u32[]{:S(2)}) copy-start(bf16[6,16,4096]{2,1,0:T(8,128)(2,1)} %param.9) | copy-start | bytes 2359300
  1.9 0.7 %copy-start.1 = (s32[4,128]{1,0:T(4,128)S(1)}, s32[4,128]{1,0:T(4,128)}, u32[]{:S(2)}) copy-start(s32[4,128]{1,0:T(4,128)} %send_list.1) | copy-start | bytes 6148
  5.0 15.2 %collective-permute-start = (bf16[128,128]{1,0:T(8,128)(2,1)S(1)}, bf16[128,128]{1,0:T(8,128)(2,1)S(1)}, u32[]{:S(2)}, u32[]{:S(2)}) collective-permute-start(bf16[128,128]{1,0:T(8,128)(2,1)S(1)} %get-tuple-element.11), channel_id=1, source_target_pairs={{0,4},{4,0},{8,12},{12,8},{16,20},{20,16},{24,28},{28,24},{32,36},... | collective-permute-start | bytes 98312 | tf_op jit(solution)/shard_map/ppermute | solution.py:227
  5.1 15.1 %collective-permute-start.1 = (bf16[128,128]{1,0:T(8,128)(2,1)S(1)}, bf16[128,128]{1,0:T(8,128)(2,1)S(1)}, u32[]{:S(2)}, u32[]{:S(2)}) collective-permute-start(bf16[128,128]{1,0:T(8,128)(2,1)S(1)} %get-tuple-element.12), channel_id=1, source_target_pairs={{4,8},{8,4},{12,16},{16,12},{20,24},{24,20},{28,32},{32,28},{36,40... | collective-permute-start | bytes 98312 | tf_op jit(solution)/shard_map/ppermute | solution.py:227
  13.2 7.0 %collective-permute-start.2 = (bf16[128,128]{1,0:T(8,128)(2,1)S(1)}, bf16[128,128]{1,0:T(8,128)(2,1)S(1)}, u32[]{:S(2)}, u32[]{:S(2)}) collective-permute-start(bf16[128,128]{1,0:T(8,128)(2,1)S(1)} %get-tuple-element.13), channel_id=1, source_target_pairs={{0,8},{8,0},{4,12},{12,4},{16,24},{24,16},{20,28},{28,20},{32,40},... | collective-permute-start | bytes 98312 | tf_op jit(solution)/shard_map/ppermute | solution.py:236
  13.3 7.9 %collective-permute-start.3 = (bf16[128,128]{1,0:T(8,128)(2,1)S(1)}, bf16[128,128]{1,0:T(8,128)(2,1)S(1)}, u32[]{:S(2)}, u32[]{:S(2)}) collective-permute-start(bf16[128,128]{1,0:T(8,128)(2,1)S(1)} %get-tuple-element.14), channel_id=1, source_target_pairs={{8,16},{16,8},{12,20},{20,12},{24,32},{32,24},{28,36},{36,28},{40,... | collective-permute-start | bytes 98312 | tf_op jit(solution)/shard_map/ppermute | solution.py:236
  45.5 4.1 %collective-permute-start.4 = (f32[16,128]{1,0:T(8,128)S(1)}, f32[16,128]{1,0:T(8,128)S(1)}, u32[]{:S(2)}, u32[]{:S(2)}) collective-permute-start(f32[16,128]{1,0:T(8,128)S(1)} %get-tuple-element.16), channel_id=1, source_target_pairs={{0,4},{4,0},{8,12},{12,8},{16,20},{20,16},{24,28},{28,24},{32,36},... | collective-permute-start | bytes 24584 | tf_op jit(solution)/shard_map/ppermute | solution.py:227
  45.6 7.1 %collective-permute-start.5 = (f32[16,128]{1,0:T(8,128)S(1)}, f32[16,128]{1,0:T(8,128)S(1)}, u32[]{:S(2)}, u32[]{:S(2)}) collective-permute-start(f32[16,128]{1,0:T(8,128)S(1)} %get-tuple-element.17), channel_id=1, source_target_pairs={{4,8},{8,4},{12,16},{16,12},{20,24},{24,20},{28,32},{32,28},{36,40... | collective-permute-start | bytes 24584 | tf_op jit(solution)/shard_map/ppermute | solution.py:227
  53.3 4.7 %collective-permute-start.6 = (f32[128]{0:T(128)S(1)}, f32[128]{0:T(128)S(1)}, u32[]{:S(2)}, u32[]{:S(2)}) collective-permute-start(f32[128]{0:T(128)S(1)} %get-tuple-element.18), channel_id=1, source_target_pairs={{0,1},{1,0},{2,3},{3,2},{4,5},{5,4},{6,7},{7,6},{8,9},{9,8},{10,11... | collective-permute-start | bytes 1544 | tf_op jit(solution)/shard_map/ppermute | solution.py:261
  54.9 5.0 %collective-permute-start.7 = (f32[128]{0:T(128)S(1)}, f32[128]{0:T(128)S(1)}, u32[]{:S(2)}, u32[]{:S(2)}) collective-permute-start(f32[128]{0:T(128)S(1)} %get-tuple-element.18), channel_id=1, source_target_pairs={{0,2},{1,3},{2,0},{3,1},{4,6},{5,7},{6,4},{7,5},{8,10},{9,11},{10,... | collective-permute-start | bytes 1544 | tf_op jit(solution)/shard_map/ppermute | solution.py:261
  57.8 4.8 %collective-permute-start.8 = (f32[128]{0:T(128)S(1)}, f32[128]{0:T(128)S(1)}, u32[]{:S(2)}, u32[]{:S(2)}) collective-permute-start(f32[128]{0:T(128)S(1)} %get-tuple-element.18), channel_id=1, source_target_pairs={{0,3},{1,2},{2,1},{3,0},{4,7},{5,6},{6,5},{7,4},{8,11},{9,10},{10,... | collective-permute-start | bytes 1544 | tf_op jit(solution)/shard_map/ppermute | solution.py:261

commit v5 on v4

--- a/solution.py
+++ b/solution.py
@@ -66,7 +66,7 @@
         lax.fori_loop(0, SLOTS // 16, rows16, 0, unroll=2)
 
 
-def main_kernel(rows_in, ghost0, ghost1, ghost2, ghost3, order, stiff, mass_ref, minus_areas, lam, connect, var,
+def main_kernel(rows_in, ghost0, ghost1, ghost2, ghost3, order, stiff, mass_ref, factors, connect,
                 own, near, far, stage, weights, table, gather_a, gather_b, f_bufs, s_bufs, u_bufs, mass_rows, masses,
                 index_a, index_b, stiff_near, energies, blocks, stiff_sem, index_sem):
     nodes = rows_in.shape[0]
@@ -134,8 +134,8 @@
                     acc = acc + s_buf[i * 24 + j:i * 24 + j + 1, :] * u[j]
                 total = acc * u[i] if total is None else total + acc * u[i]
             halves.append(total)
-        area = minus_areas[pl.ds(n * TILES + q, 1), :]
-        energies[n, q] = jnp.concatenate(halves, axis=0) + lam[...] * area * masses[q]
+        area = factors[pl.ds(16 + n * TILES + q, 1), :]
+        energies[n, q] = jnp.concatenate(halves, axis=0) + factors[0:16, :] * area * masses[q]
 
     def add_blocks(n):
         values = jnp.concatenate([pieces(energies[n, q]) for q in range(TILES)], axis=0)
@@ -174,7 +174,7 @@
     add_blocks(chunks - 1)
     for slot in range(2):
         index_copy(0, slot).wait()
-    columns = (iota((3 * VAR_DEV, 128), 0) == var[...]).astype(bf16)
+    columns = (iota((3 * VAR_DEV, 128), 0) == factors[16 + chunks * TILES:17 + chunks * TILES, :].astype(jnp.int32)).astype(bf16)
     window = lax.dot_general(pieces(blocks[...]), columns, NT, preferred_element_type=f32)
     window = window[0:16] + window[16:32] + window[32:48]
     for part, out in enumerate((own, near, far)):
@@ -195,12 +195,12 @@
     )(modes, send_list, order)
 
 
-def main_call(rows, ghosts, order, stiff, mass_ref, minus_areas, lam, connect, var):
+def main_call(rows, ghosts, order, stiff, mass_ref, factors, connect):
     chunks = connect.shape[1] // CHUNK
     return pl.pallas_call(
         main_kernel,
         out_shape=[jax.ShapeDtypeStruct((16, VAR_DEV), f32)] * 3,
-        in_specs=[VM, VM, VM, VM, VM, SM, HB, VM, VM, VM, HB, VM], out_specs=[VM] * 3,
+        in_specs=[VM, VM, VM, VM, VM, SM, HB, VM, VM, HB], out_specs=[VM] * 3,
         scratch_shapes=[
             pltpu.VMEM((96, 128), f32), pltpu.VMEM((512, 512), bf16),
             pltpu.VMEM((rows.shape[0] + 4 * SLOTS, 128), f32),
@@ -213,7 +213,7 @@
             pltpu.SemaphoreType.DMA((chunks * TILES,)), pltpu.SemaphoreType.DMA((2,)),
         ],
         compiler_params=pltpu.CompilerParams(vmem_limit_bytes=50 * 2**20),
-    )(rows, *ghosts, order, stiff, mass_ref, minus_areas, lam, connect, var)
+    )(rows, *ghosts, order, stiff, mass_ref, factors, connect)
 
 
 OFFSETS = (1, -1, 2, -2)
@@ -252,10 +252,12 @@
     step = block_var // VAR_DEV - region
     place = jnp.where(step == 0, 0, jnp.where(step == 1 - 2 * odd, 1, 2))
     column = block_var % VAR_DEV + VAR_DEV * place
+    factors = jnp.concatenate([
+        jnp.broadcast_to(eigenvalues[:, None], (mode_dev, 128)), -areas.reshape(elem_count // 128, 128),
+        column.reshape(1, elem_count // 32).astype(f32)], axis=0)
     own, sent_a, sent_b = main_call(
-        rows, received, order, stiffness, mass_ref.transpose(0, 1, 3, 2).astype(f32),
-        -areas.reshape(elem_count // 128, 128), jnp.broadcast_to(eigenvalues[:, None], (mode_dev, 128)),
-        jnp.minimum(connect, node_count + 4 * SLOTS - 1), column.reshape(1, elem_count // 32))
+        rows, received, order, stiffness, mass_ref.transpose(0, 1, 3, 2).astype(f32), factors,
+        jnp.minimum(connect, node_count + 4 * SLOTS - 1))
     sens = own + swap(sent_a, "region", 0) + swap(sent_b, "region", 1)
     weighted = jnp.sum(mode_weight[:, None] * sens, axis=0)
     other = [lax.ppermute(weighted, "mode", [(q, q ^ by) for q in range(4)]) for by in (1, 2, 3)]

time: 63.4 us -> 62.7 us (0.989)
  waiting for transfers between devices: 8.59 us -> 7.86 us
    ppermute x2, waiting for transfers between devices: 0.98 us -> 0.25 us  [swap_two(): return lax.ppermute(array, axis, pairs)]
    broadcast_in_dim x1 -> x0, local copies, waits for them, and re-layouts: 0.72 us -> none  [shards(): jnp.broadcast_to(eigenvalues[:, None], (mode_dev, 128))]
    convert_element_type x0 -> x1, other arithmetic: none -> 0.67 us  [shards(): column.reshape(1, elem_count // 32).astype(f32)]
    reshape x1 -> x0, other arithmetic: 0.67 us -> none  [shards(): column.reshape(1, elem_count // 32)]
    concatenate x0 -> x1, local copies, waits for them, and re-layouts: none -> 0.66 us  [shards(): jnp.concatenate([jnp.broadcast_to(eigenvalues[:, None], (mode_dev, 128)),...]
  transfers between devices with their start and end apart: 9 -> 9, of which waited for: 4 -> 4; matrix products, arithmetic and copies ran while one was open for 5% -> 6% of each run, Pallas kernels for 0% -> 0%
where the time goes in v5:
time: 62.7 us; the launch traced here: 62.3 us
  Pallas kernels  25.9 us (41%)
  starting transfers between devices  21 us (33%)
  waiting for transfers between devices  7.86 us (13%)
  other arithmetic  4.27 us (7%)
  local copies, waits for them, and re-layouts  2.48 us (4%)
  between operations  0.78 us (1%)
    pallas_call x1, Pallas kernels, main_call(): pl.pallas_call(main_kernel, out_shape=[jax.ShapeDtypeStruct((16, VAR_DEV)...  23.5 us
    ppermute x4, starting transfers between devices, swap(): return lax.ppermute(array, axis, pairs)  12.3 us
    ppermute x3, starting transfers between devices, shards(): lax.ppermute(weighted, 'mode', [(q, q ^ by) for q in range(4)])  4.7 us
    ppermute x3, waiting for transfers between devices, shards(): lax.ppermute(weighted, 'mode', [(q, q ^ by) for q in range(4)])  4.54 us
    ppermute x2, starting transfers between devices, swap_two(): return lax.ppermute(array, axis, pairs)  3.99 us
    ppermute x4, waiting for transfers between devices, swap(): return lax.ppermute(array, axis, pairs)  3.07 us
    pallas_call x1, Pallas kernels, send_rows(): pl.pallas_call(send_kernel, out_shape=[jax.ShapeDtypeStruct((SLOTS, 128),...  2.37 us
    unnamed x6, local copies, waits for them, and re-layouts  1.82 us
  transfers between devices with their start and end apart: 9, of which 4 were waited for; matrix products, arithmetic and copies ran while one was open for 6% of the time, Pallas kernels for 0%

profile of v5, /device:TPU:6, one launch (start us, length us, event | category | flops | bytes accessed | tf_op | source)
XLA Modules:
  0.0 62.3 jit_solution(10481862368637634337)
XLA Ops:
  0.6 0.0 copy-start.2
  0.7 0.1 pad_add_fusion.order
  0.8 0.0 copy-start
  0.8 1.1 %copy-done = bf16[6,16,4096]{2,1,0:T(8,128)(2,1)S(1)} copy-done((bf16[6,16,4096]{2,1,0:T(8,128)(2,1)S(1)}, bf16[6,16,4096]{2,1,0:T(8,128)(2,1)}, u32[]{:S(2)}) %copy-start) | copy-done | bytes 786456
  1.9 0.0 copy-start.1
  1.9 0.7 %copy-done.1 = s32[4,128]{1,0:T(4,128)S(1)} copy-done((s32[4,128]{1,0:T(4,128)S(1)}, s32[4,128]{1,0:T(4,128)}, u32[]{:S(2)}) %copy-start.1) | copy-done | bytes 2072
  2.6 2.4 %shard_map.104 = (bf16[128,128]{1,0:T(8,128)(2,1)S(1)}, bf16[128,128]{1,0:T(8,128)(2,1)S(1)}, bf16[128,128]{1,0:T(8,128)(2,1)S(1)}, bf16[128,128]{1,0:T(8,128)(2,1)S(1)}, f32[4096,128]{1,0:T(8,128)S(1)}) custom-call(bf16[96,4096]{1,0:T(8,128)(2,1)S(1)} %bitcast.11, s32[4,128]{1,0:T(4,128)S(1)} %copy-done.1, s32[4]{0:T(128)S(1)} %pad_add_fusion.order), custom_call_target="tpu_custom_call" | custom-call | tf_op jit(solution)/shard_map/pallas_call | solution.py:190
  5.0 0.1 collective-permute-start
  5.1 8.1 %collective-permute-start.1 = (bf16[128,128]{1,0:T(8,128)(2,1)S(1)}, bf16[128,128]{1,0:T(8,128)(2,1)S(1)}, u32[]{:S(2)}, u32[]{:S(2)}) collective-permute-start(bf16[128,128]{1,0:T(8,128)(2,1)S(1)} %get-tuple-element.12), channel_id=1, source_target_pairs={{4,8},{8,4},{12,16},{16,12},{20,24},{24,20},{28,32},{32,28},{36,40... | collective-permute-start | bytes 98312 | tf_op jit(solution)/shard_map/ppermute | solution.py:227
  13.2 0.1 collective-permute-start.2
  13.3 3.9 %collective-permute-start.3 = (bf16[128,128]{1,0:T(8,128)(2,1)S(1)}, bf16[128,128]{1,0:T(8,128)(2,1)S(1)}, u32[]{:S(2)}, u32[]{:S(2)}) collective-permute-start(bf16[128,128]{1,0:T(8,128)(2,1)S(1)} %get-tuple-element.14), channel_id=1, source_target_pairs={{8,16},{16,8},{12,20},{20,12},{24,32},{32,24},{28,36},{36,28},{40,... | collective-permute-start | bytes 98312 | tf_op jit(solution)/shard_map/ppermute | solution.py:236
  17.2 0.7 %negate_bitcast_fusion = f32[32,128]{1,0:T(8,128)S(1)} fusion(f32[4096]{0:T(1024)} %param.12), kind=kLoop, calls=%fused_computation.3 | loop fusion | flops 4096 | bytes 32768 | tf_op jit(solution)/shard_map/neg | solution.py:256
  17.9 0.9 %broadcast_minimum_fusion.connect = s32[4,4096]{1,0:T(4,128)S(1)} fusion(s32[4,4096]{1,0:T(4,128)} %param.15), kind=kLoop, calls=%fused_computation.1 | loop fusion | flops 16384 | bytes 131072 | tf_op jit(solution)/shard_map/min | solution.py:260
  18.8 0.7 %convert_bitcast_fusion.mass_ref = f32[6,4,4,6]{3,2,1,0:T(4,128)S(1)} fusion(bf16[6,4,6,4]{2,3,1,0:T(4,128)(2,1)} %param.11), kind=kLoop, calls=%fused_computation | loop fusion | flops 576 | bytes 3456 | tf_op jit(solution)/shard_map/convert_element_type | solution.py:259
  19.5 0.7 %convert_bitcast_fusion.1 = f32[1,128]{1,0:T(1,128)S(1)} fusion(s32[128]{0:T(128)} %param.16, s32[]{:T(128)S(6)} %sub.31, s32[]{:T(128)S(6)} %axis_index.15), kind=kLoop, calls=%fused_computation.17 | loop fusion | flops 3456 | bytes 1032 | tf_op jit(solution)/shard_map/convert_element_type | solution.py:257
  20.2 0.7 %pad.clone = f32[49]{0:T(128)S(1)} pad(f32[16]{0:T(128)} %param.13, f32[]{:T(128)} %constant.69), padding=0_33 | pad | bytes 264 | tf_op jit(solution)/shard_map/concatenate | solution.py:255
  20.8 0.1 pad_maximum_fusion.factors
  20.9 0.0 collective-permute-done.ghost0
  20.9 0.0 collective-permute-done.1.ghost1
  20.9 0.0 collective-permute-done.2.ghost2
  20.9 0.2 collective-permute-done.3.ghost3
  21.2 23.5 %shard_map.105 = (f32[16,128]{1,0:T(8,128)S(1)}, f32[16,128]{1,0:T(8,128)S(1)}, f32[16,128]{1,0:T(8,128)S(1)}) custom-call(f32[4096,128]{1,0:T(8,128)S(1)} %get-tuple-element.10.rows_in, bf16[128,128]{1,0:T(8,128)(2,1)S(1)} %collective-permute-done.ghost0, bf16[128,128]{1,0:T(8,128)(2,1)S(1)} %collective-permute-done.1.ghost1, ...), custom_call_target="tpu_custom_call" | custom-call | tf_op jit(solution)/shard_map/pallas_call | solution.py:200
  44.7 0.1 collective-permute-start.4
  44.8 4.0 %collective-permute-start.5 = (f32[16,128]{1,0:T(8,128)S(1)}, f32[16,128]{1,0:T(8,128)S(1)}, u32[]{:S(2)}, u32[]{:S(2)}) collective-permute-start(f32[16,128]{1,0:T(8,128)S(1)} %get-tuple-element.17), channel_id=1, source_target_pairs={{4,8},{8,4},{12,16},{16,12},{20,24},{24,20},{28,32},{32,28},{36,40... | collective-permute-start | bytes 24584 | tf_op jit(solution)/shard_map/ppermute | solution.py:227
  48.9 0.0 collective-permute-done.4
  48.9 3.1 %collective-permute-done.5 = f32[16,128]{1,0:T(8,128)S(1)} collective-permute-done((f32[16,128]{1,0:T(8,128)S(1)}, f32[16,128]{1,0:T(8,128)S(1)}, u32[]{:S(2)}, u32[]{:S(2)}) %collective-permute-start.5) | collective-permute-done | bytes 8224 | tf_op jit(solution)/shard_map/ppermute | solution.py:227
  51.9 0.0 copy-done.2
  51.9 0.6 multiply_reduce_fusion
  52.5 1.6 %collective-permute-start.6 = (f32[128]{0:T(128)S(1)}, f32[128]{0:T(128)S(1)}, u32[]{:S(2)}, u32[]{:S(2)}) collective-permute-start(f32[128]{0:T(128)S(1)} %get-tuple-element.18), channel_id=1, source_target_pairs={{0,1},{1,0},{2,3},{3,2},{4,5},{5,4},{6,7},{7,6},{8,9},{9,8},{10,11... | collective-permute-start | bytes 1544 | tf_op jit(solution)/shard_map/ppermute | solution.py:263
  54.1 2.9 %collective-permute-start.7 = (f32[128]{0:T(128)S(1)}, f32[128]{0:T(128)S(1)}, u32[]{:S(2)}, u32[]{:S(2)}) collective-permute-start(f32[128]{0:T(128)S(1)} %get-tuple-element.18), channel_id=1, source_target_pairs={{0,2},{1,3},{2,0},{3,1},{4,6},{5,7},{6,4},{7,5},{8,10},{9,11},{10,... | collective-permute-start | bytes 1544 | tf_op jit(solution)/shard_map/ppermute | solution.py:263
  57.0 0.2 collective-permute-start.8
  57.2 0.0 collective-permute-done.6
  57.2 1.9 %collective-permute-done.7 = f32[128]{0:T(128)S(1)} collective-permute-done((f32[128]{0:T(128)S(1)}, f32[128]{0:T(128)S(1)}, u32[]{:S(2)}, u32[]{:S(2)}) %collective-permute-start.7) | collective-permute-done | bytes 544 | tf_op jit(solution)/shard_map/ppermute | solution.py:263
  59.2 2.6 %collective-permute-done.8 = f32[128]{0:T(128)S(1)} collective-permute-done((f32[128]{0:T(128)S(1)}, f32[128]{0:T(128)S(1)}, u32[]{:S(2)}, u32[]{:S(2)}) %collective-permute-start.8) | collective-permute-done | bytes 544 | tf_op jit(solution)/shard_map/ppermute | solution.py:263
  61.8 0.5 add_add_fusion.1
Async XLA Ops:
  0.6 51.3 %copy-start.2 = (f32[16]{0:T(128)S(1)}, f32[16]{0:T(128)}, u32[]{:S(2)}) copy-start(f32[16]{0:T(128)} %param.17) | copy-start | bytes 196
  0.8 1.1 %copy-start = (bf16[6,16,4096]{2,1,0:T(8,128)(2,1)S(1)}, bf16[6,16,4096]{2,1,0:T(8,128)(2,1)}, u32[]{:S(2)}) copy-start(bf16[6,16,4096]{2,1,0:T(8,128)(2,1)} %param.9) | copy-start | bytes 2359300
  1.9 0.7 %copy-start.1 = (s32[4,128]{1,0:T(4,128)S(1)}, s32[4,128]{1,0:T(4,128)}, u32[]{:S(2)}) copy-start(s32[4,128]{1,0:T(4,128)} %send_list.1) | copy-start | bytes 6148
  5.0 16.0 %collective-permute-start = (bf16[128,128]{1,0:T(8,128)(2,1)S(1)}, bf16[128,128]{1,0:T(8,128)(2,1)S(1)}, u32[]{:S(2)}, u32[]{:S(2)}) collective-permute-start(bf16[128,128]{1,0:T(8,128)(2,1)S(1)} %get-tuple-element.11), channel_id=1, source_target_pairs={{0,4},{4,0},{8,12},{12,8},{16,20},{20,16},{24,28},{28,24},{32,36},... | collective-permute-start | bytes 98312 | tf_op jit(solution)/shard_map/ppermute | solution.py:227
  5.1 15.9 %collective-permute-start.1 = (bf16[128,128]{1,0:T(8,128)(2,1)S(1)}, bf16[128,128]{1,0:T(8,128)(2,1)S(1)}, u32[]{:S(2)}, u32[]{:S(2)}) collective-permute-start(bf16[128,128]{1,0:T(8,128)(2,1)S(1)} %get-tuple-element.12), channel_id=1, source_target_pairs={{4,8},{8,4},{12,16},{16,12},{20,24},{24,20},{28,32},{32,28},{36,40... | collective-permute-start | bytes 98312 | tf_op jit(solution)/shard_map/ppermute | solution.py:227
  13.2 7.8 %collective-permute-start.2 = (bf16[128,128]{1,0:T(8,128)(2,1)S(1)}, bf16[128,128]{1,0:T(8,128)(2,1)S(1)}, u32[]{:S(2)}, u32[]{:S(2)}) collective-permute-start(bf16[128,128]{1,0:T(8,128)(2,1)S(1)} %get-tuple-element.13), channel_id=1, source_target_pairs={{0,8},{8,0},{4,12},{12,4},{16,24},{24,16},{20,28},{28,20},{32,40},... | collective-permute-start | bytes 98312 | tf_op jit(solution)/shard_map/ppermute | solution.py:236
  13.3 7.9 %collective-permute-start.3 = (bf16[128,128]{1,0:T(8,128)(2,1)S(1)}, bf16[128,128]{1,0:T(8,128)(2,1)S(1)}, u32[]{:S(2)}, u32[]{:S(2)}) collective-permute-start(bf16[128,128]{1,0:T(8,128)(2,1)S(1)} %get-tuple-element.14), channel_id=1, source_target_pairs={{8,16},{16,8},{12,20},{20,12},{24,32},{32,24},{28,36},{36,28},{40,... | collective-permute-start | bytes 98312 | tf_op jit(solution)/shard_map/ppermute | solution.py:236
  44.7 4.1 %collective-permute-start.4 = (f32[16,128]{1,0:T(8,128)S(1)}, f32[16,128]{1,0:T(8,128)S(1)}, u32[]{:S(2)}, u32[]{:S(2)}) collective-permute-start(f32[16,128]{1,0:T(8,128)S(1)} %get-tuple-element.16), channel_id=1, source_target_pairs={{0,4},{4,0},{8,12},{12,8},{16,20},{20,16},{24,28},{28,24},{32,36},... | collective-permute-start | bytes 24584 | tf_op jit(solution)/shard_map/ppermute | solution.py:227
  44.8 7.1 %collective-permute-start.5 = (f32[16,128]{1,0:T(8,128)S(1)}, f32[16,128]{1,0:T(8,128)S(1)}, u32[]{:S(2)}, u32[]{:S(2)}) collective-permute-start(f32[16,128]{1,0:T(8,128)S(1)} %get-tuple-element.17), channel_id=1, source_target_pairs={{4,8},{8,4},{12,16},{16,12},{20,24},{24,20},{28,32},{32,28},{36,40... | collective-permute-start | bytes 24584 | tf_op jit(solution)/shard_map/ppermute | solution.py:227
  52.5 4.7 %collective-permute-start.6 = (f32[128]{0:T(128)S(1)}, f32[128]{0:T(128)S(1)}, u32[]{:S(2)}, u32[]{:S(2)}) collective-permute-start(f32[128]{0:T(128)S(1)} %get-tuple-element.18), channel_id=1, source_target_pairs={{0,1},{1,0},{2,3},{3,2},{4,5},{5,4},{6,7},{7,6},{8,9},{9,8},{10,11... | collective-permute-start | bytes 1544 | tf_op jit(solution)/shard_map/ppermute | solution.py:263
  54.1 5.0 %collective-permute-start.7 = (f32[128]{0:T(128)S(1)}, f32[128]{0:T(128)S(1)}, u32[]{:S(2)}, u32[]{:S(2)}) collective-permute-start(f32[128]{0:T(128)S(1)} %get-tuple-element.18), channel_id=1, source_target_pairs={{0,2},{1,3},{2,0},{3,1},{4,6},{5,7},{6,4},{7,5},{8,10},{9,11},{10,... | collective-permute-start | bytes 1544 | tf_op jit(solution)/shard_map/ppermute | solution.py:263
  57.0 4.8 %collective-permute-start.8 = (f32[128]{0:T(128)S(1)}, f32[128]{0:T(128)S(1)}, u32[]{:S(2)}, u32[]{:S(2)}) collective-permute-start(f32[128]{0:T(128)S(1)} %get-tuple-element.18), channel_id=1, source_target_pairs={{0,3},{1,2},{2,1},{3,0},{4,7},{5,6},{6,5},{7,4},{8,11},{9,10},{10,... | collective-permute-start | bytes 1544 | tf_op jit(solution)/shard_map/ppermute | solution.py:263
